TPU v7x, 128 devices: a whole 4x4x4 slice. The times are simulated.
128 devices in a mesh: sens: 4 (over y_hi, core), par: 32 (over y_lo, z, x).
Axes of the slice: x: 4, y: 4 (y_hi: 2, y_lo: 2; y = y_hi * 2 + y_lo), z: 4, core: 2. Of those that a mesh axis runs over, the one named last changes fastest.
Arguments:
- probes: float32 [2048, 512], P('par', 'sens'), may hold values from -6 to 6
- kernel: float32 [64, 2048, 2048], P(None, 'par', 'sens'), may hold values from -0.015625 to 0.015625
- noise_inverse: float32 [64, 64], replicated, may hold values from -1 to 3, as said below
- sensor_weight: float32 [2048], P('sens'), may hold values from 0.25 to 4
Outputs:
- hessian_action: float32 [2048, 512], P('par', 'sens')
Inputs may be any that keep to these rules, and one draw needn't show every extreme that they name: `noise_inverse`: symmetric.
All inputs are finite; a program needn't handle non-finite values.
Results may differ from a plain program's by a relative error of at most 0.0001.
Values sent between devices are 32-bit elements; how exact they have to be, the bound alone decides.
No kernel may reach another device: no remote copies, remote signals or barrier semaphores. Data moves between devices by JAX's collectives and lax.ppermute only.
A program may use at most 128 MiB of HBM per device.

v0:
```python
import jax
import jax.numpy as jnp
from jax import lax
from jax.sharding import PartitionSpec as P


def apply_noise(observed, noise_inverse, weights_part):
    time_steps = noise_inverse.shape[0]
    row_count = observed.shape[0]
    columns = observed.shape[1]
    probe_count = columns // time_steps
    mixed = jnp.einsum(
        "tu,rup->rtp",
        noise_inverse,
        observed.reshape(row_count, time_steps, probe_count),
        precision=lax.Precision.HIGHEST,
        preferred_element_type=jnp.float32,
    )
    return mixed.reshape(row_count, columns) * weights_part[:, None]


def per_device(probes, kernel, noise_inverse, sensor_weight):
    highest = lax.Precision.HIGHEST
    time_steps = noise_inverse.shape[0]
    par_rows = kernel.shape[1]
    sensor_rows = kernel.shape[2]
    gathered = lax.all_gather(probes, "sens", axis=1, tiled=True)
    columns = gathered.shape[1]
    probe_count = columns // time_steps
    lag_list = jnp.arange(time_steps, dtype=jnp.int32)
    probe_field = gathered.reshape(par_rows, time_steps, probe_count)
    padded = jnp.pad(probe_field, ((0, 0), (time_steps, 0), (0, 0)))
    shifted = jax.vmap(
        lambda lag_index: lax.dynamic_slice_in_dim(padded, time_steps - lag_index, time_steps, 1)
    )(lag_list)
    shifted = shifted.reshape(time_steps * par_rows, columns)
    kernel_flat = kernel.reshape(time_steps * par_rows, sensor_rows)
    observed = lax.psum(
        lax.dot_general(
            kernel_flat,
            shifted,
            (((0,), (0,)), ((), ())),
            precision=highest,
            preferred_element_type=jnp.float32,
        ),
        "par",
    )
    weighted = apply_noise(observed, noise_inverse, sensor_weight)
    spread = jnp.dot(kernel_flat, weighted, precision=highest, preferred_element_type=jnp.float32)
    spread = spread.reshape(time_steps, par_rows, time_steps, probe_count)
    spread = jnp.pad(spread, ((0, 0), (0, 0), (0, time_steps), (0, 0)))
    earlier = jax.vmap(
        lambda lag_index, spread_lag: lax.dynamic_slice_in_dim(spread_lag, lag_index, time_steps, 1)
    )(lag_list, spread)
    partial_action = jnp.sum(earlier, axis=0).reshape(par_rows, columns)
    return lax.psum_scatter(partial_action, "sens", scatter_dimension=1, tiled=True)


def solution(mesh):
    placed = (P("par", "sens"), P(None, "par", "sens"), P(), P("sens"))
    return jax.shard_map(
        per_device, mesh=mesh, in_specs=placed, out_specs=P("par", "sens"), check_vma=False
    )
```

profile of v0, /device:TPU:0, one launch (start us, length us, event | category | flops | bytes accessed | tf_op | source)
XLA Modules:
  0.0 506.8 jit_solution(11033631472231549989)
XLA Ops:
  6.5 0.0 copy-start
  6.5 0.0 all-reduce.4.cloned.1.call-start
  6.5 7.1 %all_gather.3 = f32[64,512]{1,0:T(8,128)S(1)} all-gather(f32[64,128]{1,0:T(8,128)} %param.4), channel_id=1, replica_groups=mesh['sens'=4,'par'=32] {'sens'}, dimensions={1}, use_global_device_ids=true | all-gather | bytes 163840 | tf_op jit(solution)/shard_map/all_gather | solution.py:27
  13.7 0.1 copy.8
  13.9 7.4 %gather_fusion = f32[64,64,64,8]{1,3,2,0:T(8,128)} fusion(f32[64,128,8]{0,2,1:T(8,128)S(1)} %pad.8, s32[64]{0:T(128)S(1)} %fusion.6), kind=kCustom, calls=%fused_computation | custom fusion | bytes 16777984 | tf_op jit(solution)/shard_map/vmap()/gather | solution.py:34
  21.2 17.7 %copy.9 = f32[64,64,64,8]{1,0,3,2:T(8,128)} copy(f32[64,64,64,8]{1,3,2,0:T(8,128)} %gather_fusion) | data formatting | bytes 16777216 | tf_op jit(solution)/shard_map/vmap()/gather | solution.py:34
  39.0 14.7 %reshape.46 = f32[4096,512]{0,1:T(8,128)} reshape(f32[64,64,64,8]{1,0,3,2:T(8,128)} %copy.9) | data formatting | bytes 16777216 | tf_op jit(solution)/shard_map/reshape | solution.py:36
  53.7 16.4 %convolution_bitcast_fusion.1 = f32[512,64,8]{0,2,1:T(8,128)S(1)} fusion(f32[4096,512]{0,1:T(8,128)} %reshape.46, f32[4096,512]{1,0:T(8,128)} %bitcast.31), kind=kOutput, calls=%fused_computation.5 | convolution fusion | flops 12884901888 | bytes 17825792 | tf_op jit(solution)/shard_map/dot_general | solution.py:39
  70.1 1.6 copy.10
  71.7 0.0 all-reduce.4.cloned.1.call-update
  71.8 0.0 reduce-scatter.2.cloned.1.call-start
  71.8 312.0 %all-reduce.4.cloned.1.call-done = f32[512,64,8]{0,1,2:T(8,128)} async-done(((f32[512,64,8]{0,1,2:T(8,128)}), f32[512,64,8]{0,1,2:T(8,128)}) %all-reduce.4.cloned.1.call-update) | async-done | bytes 1048592 | tf_op jit(solution)/shard_map/psum | solution.py:38
  383.8 0.0 copy-done
  383.8 0.0 copy-done.2
  383.8 2.3 fusion
  386.1 19.6 %convolution_bitcast_fusion = f32[4096,512]{0,1:T(8,128)} fusion(f32[4096,512]{1,0:T(8,128)} %bitcast.32, f32[512,64,8]{0,1,2:T(8,128)S(1)} %fusion), kind=kOutput, calls=%fused_computation.2 | convolution fusion | flops 12884901888 | bytes 17825792 | tf_op jit(solution)/shard_map/dot_general | solution.py:49
  405.7 14.2 %reshape.49 = f32[64,64,64,8]{1,0,3,2:T(8,128)} reshape(f32[4096,512]{0,1:T(8,128)} %convolution_bitcast_fusion) | data formatting | bytes 16777216 | tf_op jit(solution)/shard_map/reshape | solution.py:50
  419.9 18.6 %copy.12 = f32[64,64,64,8]{1,3,0,2:T(8,128)S(1)} copy(f32[64,64,64,8]{1,0,3,2:T(8,128)} %reshape.49) | data formatting | bytes 16777216 | tf_op jit(solution)/shard_map/reshape | solution.py:50
  438.5 11.2 %pad.9 = f32[64,64,128,8]{1,3,0,2:T(8,128)} pad(f32[64,64,64,8]{1,3,0,2:T(8,128)S(1)} %copy.12, f32[]{:T(128)} %constant.4.clone.1), padding=0_0x0_0x0_64x0_0 | pad | bytes 25165828 | tf_op jit(solution)/shard_map/jit(_pad)/pad | solution.py:51
  449.8 13.5 %gather_fusion.1 = f32[64,64,64,8]{1,3,2,0:T(8,128)} fusion(f32[64,64,128,8]{1,3,0,2:T(8,128)} %pad.9, s32[64]{0:T(128)S(1)} %fusion.9), kind=kCustom, calls=%fused_computation.1 | custom fusion | bytes 16778240 | tf_op jit(solution)/shard_map/vmap()/gather | solution.py:53
  463.3 7.8 %reduce_sum.9 = f32[64,64,8]{0,2,1:T(8,128)} reduce(f32[64,64,64,8]{1,3,2,0:T(8,128)} %gather_fusion.1, f32[]{:T(128)} %constant.4.clone.1), dimensions={0}, to_apply=%region_1.2 | reduce | flops 2064384 | bytes 8519684 | tf_op jit(solution)/shard_map/reduce_sum | solution.py:55
  471.1 0.0 reduce-scatter.2.cloned.1.call-update
  471.1 27.3 %reduce-scatter.2.cloned.1.call-done = f32[64,128]{0,1:T(8,128)} async-done(((f32[64,512]{0,1:T(8,128)}), f32[64,128]{0,1:T(8,128)}) %reduce-scatter.2.cloned.1.call-update) | async-done | bytes 32784 | tf_op jit(solution)/shard_map/reduce_scatter | solution.py:56
  498.4 1.5 copy.13
  (6 shorter events, 0.1 us)
Async XLA Ops:
  6.5 377.3 %copy-start = (f32[64,64]{1,0:T(8,128)S(1)}, f32[64,64]{1,0:T(8,128)}, u32[]{:S(2)}) copy-start(f32[64,64]{1,0:T(8,128)} %param.6) | copy-start | bytes 49156
  6.5 377.3 %all-reduce.4.cloned.1.call-start = ((), (), s32[]{:S(2)}) async-start(), calls=%async_computation.1 | async-start | bytes 2097152 | tf_op jit(solution)/shard_map/psum | solution.py:38
  53.7 330.1 %copy-start.2 = (f32[512]{0:T(512)S(1)}, f32[512]{0:T(512)}, u32[]{:S(2)}) copy-start(f32[512]{0:T(512)} %param.7) | copy-start | bytes 6148
  71.8 426.7 %reduce-scatter.2.cloned.1.call-start = ((), (), s32[]{:S(2)}) async-start(), calls=%async_computation.2 | async-start | bytes 327680 | tf_op jit(solution)/shard_map/reduce_scatter | solution.py:56
  449.8 50.2 %copy-start.1 = (f32[64,64]{1,0:T(8,128)S(1)}, f32[64,64]{1,0:T(8,128)}, u32[]{:S(2)}) copy-start(f32[64,64]{1,0:T(8,128)} %param.6) | copy-start | bytes 49156
Sparse Core Ops, SparseCore 0:
  71.9 311.8 all-reduce.3
  471.2 27.1 reduce-scatter.1
where the time goes:
time: 508 us; the launch traced here: 507 us
  waiting for transfers between devices  339 us (67%)
  local copies, waits for them, and re-layouts  101 us (20%)
  matrix products  38.2 us (8%)
  between operations  13.5 us (3%)
  other arithmetic  7.83 us (2%)
  blocking collectives  7.14 us (1%)
    psum x1, waiting for transfers between devices, per_device(): lax.psum(lax.dot_general(kernel_flat, shifted, (((0,), (0,)), ((), ())),...  312 us
    reshape x2, local copies, waits for them, and re-layouts, per_device(): spread = spread.reshape(time_steps, par_rows, time_steps, probe_count)  32.8 us
    reduce_scatter x1, waiting for transfers between devices, per_device(): lax.psum_scatter(partial_action, 'sens', scatter_dimension=1, tiled=True)  27.3 us
    gather x2, local copies, waits for them, and re-layouts, per_device(): lax.dynamic_slice_in_dim(padded, time_steps - lag_index, time_steps, 1)  25.1 us
    dot_general x1, matrix products, per_device(): jnp.dot(kernel_flat, weighted, precision=highest, preferred_element_type=...  19.6 us
    dot_general x1, matrix products, per_device(): lax.dot_general(kernel_flat, shifted, (((0,), (0,)), ((), ())), precision...  16.4 us
    reshape x1, local copies, waits for them, and re-layouts, per_device(): shifted = shifted.reshape(time_steps * par_rows, columns)  14.7 us
    gather x1, local copies, waits for them, and re-layouts, per_device(): lax.dynamic_slice_in_dim(spread_lag, lag_index, time_steps, 1)  13.5 us
  transfers between devices with their start and end apart: 2, of which 2 were waited for; matrix products, arithmetic and copies ran while one was open for 0% of the time, Pallas kernels for 0%

commit v1 on v0

v1 whole, which is shorter than its diff:
```python
import jax
import jax.numpy as jnp
from jax import lax
from jax.experimental import pallas as pl
from jax.experimental.pallas import tpu as pltpu
from jax.sharding import PartitionSpec as P

F32 = jnp.float32
BF16 = jnp.bfloat16
GROUP = 4
TIERS = 4


def split(value):
    high = value.astype(BF16)
    return high, (value - high.astype(F32)).astype(BF16)


def kernel_copies(kernel_ref, held, sems, block_rows, blocks):
    return [
        pltpu.make_async_copy(
            kernel_ref.at[pl.ds(b * block_rows, block_rows)],
            held.at[pl.ds(b * block_rows, block_rows)],
            sems.at[b],
        )
        for b in range(blocks)
    ]


def wait_block(kernel_ref, held, sems, block_rows, b):
    rows = pl.ds(pl.multiple_of(b * block_rows, block_rows), block_rows)
    pltpu.make_async_copy(kernel_ref.at[rows], held.at[rows], sems.at[b]).wait()
    return rows


def forward_kernel(p0, p1, p2, p3, kernel_ref, out_ref, held, field, moved, sems):
    params, part_columns = p0.shape
    columns = out_ref.shape[0]
    block_rows = GROUP * params
    blocks = kernel_ref.shape[0] // block_rows
    step_rows = 8 * GROUP
    per_tier = blocks // TIERS
    tier_rows = columns // TIERS
    pad = tier_rows - step_rows
    for copy in kernel_copies(kernel_ref, held, sems, block_rows, blocks):
        copy.start()
    me = lax.axis_index("sens")
    field[pl.ds(0, step_rows), :] = jnp.zeros((step_rows, params), F32)
    for other, piece in enumerate((p0, p1, p2, p3)):
        start = step_rows + part_columns * jnp.bitwise_xor(me, other)
        field[pl.ds(pl.multiple_of(start, step_rows), part_columns), :] = piece[...].T
    shifted = jnp.concatenate(
        [field[pl.ds(step_rows - 8 * lag, columns), :] for lag in range(GROUP)], axis=1
    )
    high, low = split(shifted)
    moved[pl.ds(0, pad), :] = jnp.zeros((pad, 3 * block_rows), BF16)
    moved[pl.ds(pad, columns), pl.ds(0, block_rows)] = high
    moved[pl.ds(pad, columns), pl.ds(block_rows, block_rows)] = high
    moved[pl.ds(pad, columns), pl.ds(2 * block_rows, block_rows)] = low
    out_ref[...] = jnp.zeros_like(out_ref)
    for tier in range(TIERS):
        first = tier * tier_rows
        count = columns - first

        @pl.loop(0, per_tier)
        def _(i, tier=tier, first=first, count=count):
            rows = wait_block(kernel_ref, held, sems, block_rows, tier * per_tier + i)
            k_high, k_low = split(held[rows, :])
            weights = jnp.concatenate([k_high, k_low, k_high], axis=0)
            start = pl.multiple_of(pad - step_rows * i, step_rows)
            out_ref[pl.ds(first, count), :] += jnp.dot(
                moved[pl.ds(start, count), :], weights, preferred_element_type=F32
            )


def backward_kernel(
    observed, noise, sensor_weight, kernel_ref, kept, sent, held, spread, weighted, sems
):
    columns, sensors = observed.shape
    params = kept.shape[1]
    part_columns = kept.shape[2]
    time_steps = noise.shape[0]
    block_rows = GROUP * params
    blocks = kernel_ref.shape[0] // block_rows
    step_rows = 8 * GROUP
    per_tier = blocks // TIERS
    tier_rows = columns // TIERS
    pad = tier_rows - step_rows
    for copy in kernel_copies(kernel_ref, held, sems, block_rows, blocks):
        copy.start()

    row = lax.broadcasted_iota(jnp.int32, (time_steps, columns), 0)
    col = lax.broadcasted_iota(jnp.int32, (time_steps, columns), 1)
    expand = jnp.where(row == col // 8, 1.0, 0.0).astype(BF16)
    same = (
        lax.broadcasted_iota(jnp.int32, (1, 8, columns), 1)
        == lax.broadcasted_iota(jnp.int32, (1, 8, columns), 2) % 8
    )

    def widen(part):
        wide = jnp.dot(part, expand, preferred_element_type=F32)
        wide = jnp.where(same, wide[:, None, :], 0.0)
        return wide.reshape(columns, columns).astype(BF16)

    n_high, n_low = [widen(part) for part in split(noise[...])]
    o_high, o_low = split(observed[...])
    mixed = jnp.dot(n_high, o_high, preferred_element_type=F32)
    mixed += jnp.dot(n_high, o_low, preferred_element_type=F32)
    mixed += jnp.dot(n_low, o_high, preferred_element_type=F32)
    high, low = split(mixed * sensor_weight[...])
    weighted[pl.ds(0, columns), pl.ds(0, sensors)] = high
    weighted[pl.ds(0, columns), pl.ds(sensors, sensors)] = high
    weighted[pl.ds(0, columns), pl.ds(2 * sensors, sensors)] = low
    weighted[pl.ds(columns, pad), :] = jnp.zeros((pad, 3 * sensors), BF16)
    spread[...] = jnp.zeros_like(spread)
    for tier in range(TIERS):
        first = tier * tier_rows
        count = columns - first

        @pl.loop(0, per_tier)
        def _(i, tier=tier, first=first, count=count):
            rows = wait_block(kernel_ref, held, sems, block_rows, tier * per_tier + i)
            k_high, k_low = split(held[rows, :])
            weights = jnp.concatenate([k_high, k_low, k_high], axis=1)
            start = pl.multiple_of(first + step_rows * i, step_rows)
            spread[pl.ds(0, count), :] += lax.dot_general(
                weighted[pl.ds(start, count), :],
                weights,
                (((1,), (1,)), ((), ())),
                preferred_element_type=F32,
            )

    me = lax.axis_index("sens")
    for other, target in enumerate((kept.at[0], sent.at[0], kept.at[1], sent.at[1])):
        start = pl.multiple_of(part_columns * jnp.bitwise_xor(me, other), part_columns)
        total = spread[pl.ds(start, part_columns), pl.ds(0, params)]
        for lag in range(1, GROUP):
            total += spread[pl.ds(start + 8 * lag, part_columns), pl.ds(lag * params, params)]
        target[...] = total.T


def per_device(probes, kernel, noise_inverse, sensor_weight):
    time_steps, params, sensors = kernel.shape
    part_columns = probes.shape[1]
    ranks = lax.axis_size("sens")
    columns = part_columns * ranks
    blocks = time_steps // GROUP
    block_rows = GROUP * params
    par = lax.axis_size("par")
    swap_core = [(s, s ^ 1) for s in range(ranks)]
    swap_chip = [(s, s ^ 2) for s in range(ranks)]
    kernel_flat = kernel.reshape(time_steps * params, sensors)
    vmem = pl.BlockSpec(memory_space=pltpu.VMEM)
    anywhere = pl.BlockSpec(memory_space=pl.ANY)
    compiler_params = pltpu.CompilerParams(vmem_limit_bytes=40 * 1024 * 1024)
    step_rows = 8 * GROUP
    pad = columns // TIERS - step_rows

    across = lax.ppermute(probes, "sens", swap_chip)
    beside = lax.ppermute(probes, "sens", swap_core)
    diagonal = lax.ppermute(across, "sens", swap_core)

    partial = pl.pallas_call(
        forward_kernel,
        out_shape=jax.ShapeDtypeStruct((columns, sensors), F32),
        in_specs=[vmem] * 4 + [anywhere],
        out_specs=vmem,
        scratch_shapes=[
            pltpu.VMEM((time_steps * params, sensors), F32),
            pltpu.VMEM((step_rows + columns, params), F32),
            pltpu.VMEM((pad + columns, 3 * block_rows), BF16),
            pltpu.SemaphoreType.DMA((blocks,)),
        ],
        compiler_params=compiler_params,
        name="forward_map",
    )(probes, beside, across, diagonal, kernel_flat)

    pieces = lax.all_to_all(
        partial.reshape(par, columns // par, sensors), "par", 0, 0, tiled=True
    )
    share = jnp.sum(pieces, axis=0)
    observed = lax.all_to_all(
        jnp.broadcast_to(share[None], pieces.shape), "par", 0, 0, tiled=True
    ).reshape(columns, sensors)

    piece = jax.ShapeDtypeStruct((2, params, part_columns), F32)
    kept, sent = pl.pallas_call(
        backward_kernel,
        out_shape=(piece, piece),
        in_specs=[vmem] * 3 + [anywhere],
        out_specs=(vmem, vmem),
        scratch_shapes=[
            pltpu.VMEM((time_steps * params, sensors), F32),
            pltpu.VMEM((columns + step_rows, block_rows), F32),
            pltpu.VMEM((columns + pad, 3 * sensors), BF16),
            pltpu.SemaphoreType.DMA((blocks,)),
        ],
        compiler_params=compiler_params,
        name="backward_map",
    )(observed, noise_inverse, sensor_weight.reshape(1, sensors), kernel_flat)
    kept += lax.ppermute(sent, "sens", swap_core)
    return kept[0] + lax.ppermute(kept[1], "sens", swap_chip)


def solution(mesh):
    placed = (P("par", "sens"), P(None, "par", "sens"), P(), P("sens"))
    return jax.shard_map(
        per_device, mesh=mesh, in_specs=placed, out_specs=P("par", "sens"), check_vma=False
    )
```

time: 508 us -> 87.5 us (0.17)
  waiting for transfers between devices: 339 us -> 7.31 us
  local copies, waits for them, and re-layouts: 101 us -> 7.65 us
  blocking collectives: 7.14 us -> 47.2 us
  matrix products: 38.2 us -> 0 us
  Pallas kernels: 0 us -> 17.9 us
  between operations: 13.5 us -> 0.06 us
  other arithmetic: 7.83 us -> 0.7 us
  starting transfers between devices: 0.04 us -> 6.35 us
    psum x1 -> x0, waiting for transfers between devices: 312 us -> none  [per_device(): lax.psum(lax.dot_general(kernel_flat, shifted, (((0,), (0,)), ((), ())),...]
    reshape x4 -> x0, local copies, waits for them, and re-layouts: 49.2 us -> none  [the longest x2 32.8 us: per_device(): spread = spread.reshape(time_steps, par_rows, time_steps, probe_count)]
    all_to_all x0 -> x2, blocking collectives: none -> 47.2 us  [the longest x1 26.3 us: per_device(): lax.all_to_all(partial.reshape(par, columns // par, sensors), 'par', 0, 0...]
    gather x3 -> x0, local copies, waits for them, and re-layouts: 38.6 us -> none  [the longest x2 25.1 us: per_device(): lax.dynamic_slice_in_dim(padded, time_steps - lag_index, time_steps, 1)]
    dot_general x3 -> x0, matrix products: 38.2 us -> none  [the longest x1 19.6 us: per_device(): jnp.dot(kernel_flat, weighted, precision=highest, preferred_element_type=...]
    reduce_scatter x1 -> x0, waiting for transfers between devices: 27.3 us -> none  [per_device(): lax.psum_scatter(partial_action, 'sens', scatter_dimension=1, tiled=True)]
    pallas_call x0 -> x2, Pallas kernels: none -> 17.9 us  [the longest x1 9.98 us: per_device(): pl.pallas_call(backward_kernel, out_shape=(piece, piece), in_specs=[vmem]...]
    pad x2 -> x0, local copies, waits for them, and re-layouts: 11.3 us -> none  [the longest x1 11.2 us: per_device(): spread = jnp.pad(spread, ((0, 0), (0, 0), (0, time_steps), (0, 0)))]
  transfers between devices with their start and end apart: 2 -> 5, of which waited for: 2 -> 4; matrix products, arithmetic and copies ran while one was open for 0% -> 0% of each run, Pallas kernels for 0% -> 0%
where the time goes in v1:
time: 87.5 us; the launch traced here: 87.2 us
  blocking collectives  47.2 us (54%)
  Pallas kernels  17.9 us (20%)
  local copies, waits for them, and re-layouts  7.65 us (9%)
  waiting for transfers between devices  7.31 us (8%)
  starting transfers between devices  6.35 us (7%)
    all_to_all x1, blocking collectives, per_device(): lax.all_to_all(partial.reshape(par, columns // par, sensors), 'par', 0, 0...  26.3 us
    all_to_all x1, blocking collectives, per_device(): lax.all_to_all(jnp.broadcast_to(share[None], pieces.shape), 'par', 0, 0,...  21 us
    pallas_call x1, Pallas kernels, per_device(): pl.pallas_call(backward_kernel, out_shape=(piece, piece), in_specs=[vmem]...  9.98 us
    pallas_call x1, Pallas kernels, per_device(): pl.pallas_call(forward_kernel, out_shape=jax.ShapeDtypeStruct((columns, s...  7.89 us
    unnamed x10, local copies, waits for them, and re-layouts  7.53 us
    ppermute x1, starting transfers between devices, per_device(): across = lax.ppermute(probes, 'sens', swap_chip)  3.28 us
    ppermute x1, starting transfers between devices, per_device(): return kept[0] + lax.ppermute(kept[1], 'sens', swap_chip)  2.98 us
    ppermute x1, waiting for transfers between devices, per_device(): return kept[0] + lax.ppermute(kept[1], 'sens', swap_chip)  2.52 us
  transfers between devices with their start and end apart: 5, of which 4 were waited for; matrix products, arithmetic and copies ran while one was open for 0% of the time, Pallas kernels for 0%

profile of v1, /device:TPU:0, one launch (start us, length us, event | category | flops | bytes accessed | tf_op | source)
XLA Modules:
  0.0 87.2 jit_solution(13703731865509283312)
XLA Ops:
  0.0 3.3 %collective-permute-start.1 = (f32[64,128]{1,0:T(8,128)}, f32[64,128]{1,0:T(8,128)S(1)}, u32[]{:S(2)}, u32[]{:S(2)}) collective-permute-start(f32[64,128]{1,0:T(8,128)} %p0.1), channel_id=1, source_target_pairs={{0,64},{32,96},{64,0},{96,32},{1,65},{33,97},{65,1},{97,33},{2,66}... | collective-permute-start | bytes 98312 | tf_op jit(solution)/shard_map/ppermute | solution.py:159
  3.3 0.0 collective-permute-start
  3.3 2.3 %collective-permute-done.1.p2 = f32[64,128]{1,0:T(8,128)S(1)} collective-permute-done((f32[64,128]{1,0:T(8,128)}, f32[64,128]{1,0:T(8,128)S(1)}, u32[]{:S(2)}, u32[]{:S(2)}) %collective-permute-start.1) | collective-permute-done | bytes 32800 | tf_op jit(solution)/shard_map/ppermute | solution.py:159
  5.6 0.0 collective-permute-start.2
  5.6 0.0 collective-permute-done.p1
  5.6 1.2 %collective-permute-done.2.p3 = f32[64,128]{1,0:T(8,128)S(1)} collective-permute-done((f32[64,128]{1,0:T(8,128)S(1)}, f32[64,128]{1,0:T(8,128)S(1)}, u32[]{:S(2)}, u32[]{:S(2)}) %collective-permute-start.2) | collective-permute-done | bytes 32800 | tf_op jit(solution)/shard_map/ppermute | solution.py:161
  6.8 0.0 copy-start
  6.8 3.4 %copy-done = f32[64,64,512]{2,1,0:T(8,128)S(1)} copy-done((f32[64,64,512]{2,1,0:T(8,128)S(1)}, f32[64,64,512]{2,1,0:T(8,128)}, u32[]{:S(2)}) %copy-start) | copy-done | bytes 8388632
  10.2 0.0 copy-start.2
  10.2 0.8 copy-done.2
  11.0 7.9 %forward_map.1 = f32[512,512]{1,0:T(8,128)S(1)} custom-call(f32[64,128]{1,0:T(8,128)S(1)} %copy-done.2, f32[64,128]{1,0:T(8,128)S(1)} %collective-permute-done.p1, f32[64,128]{1,0:T(8,128)S(1)} %collective-permute-done.1.p2, f32[64,128]{1,0:T(8,128)S(1)} %collective-permute-done.2.p3, f32[4096,512]{1,0:T(8,128)S(1)} %bitcast.10), custom_call_target="tpu_custom_call" | custom-call | tf_op jit(solution)/shard_map/forward_map/pallas_call | solution.py:163
  18.9 26.3 %all_to_all.10 = f32[32,16,512]{2,1,0:T(8,128)S(1)} all-to-all(f32[32,16,512]{2,1,0:T(8,128)S(1)} %bitcast.12), channel_id=1, replica_groups=mesh['sens'=4,'par'=32] {'par'}, dimensions={0} | all-to-all | bytes 2097152 | tf_op jit(solution)/shard_map/all_to_all | solution.py:178
  45.2 0.1 reduce_sum.9
  45.2 0.1 broadcast_in_dim.2
  45.3 21.0 %all_to_all.11 = f32[32,16,512]{2,1,0:T(8,128)S(1)} all-to-all(f32[32,16,512]{2,1,0:T(8,128)S(1)} %broadcast_in_dim.2), channel_id=1, replica_groups=mesh['sens'=4,'par'=32] {'par'}, dimensions={0} | all-to-all | bytes 2097152 | tf_op jit(solution)/shard_map/all_to_all | solution.py:182
  66.3 0.0 copy-done.3
  66.3 0.0 copy-done.4
  66.3 3.4 %copy-done.1 = f32[64,64,512]{2,1,0:T(8,128)S(1)} copy-done((f32[64,64,512]{2,1,0:T(8,128)S(1)}, f32[64,64,512]{2,1,0:T(8,128)}, u32[]{:S(2)}) %copy-start.1) | copy-done | bytes 8388632
  69.7 10.0 %backward_map.1 = (f32[2,64,128]{2,1,0:T(8,128)S(1)}, f32[2,64,128]{2,1,0:T(8,128)S(1)}) custom-call(f32[512,512]{1,0:T(8,128)S(1)} %bitcast.13, f32[64,64]{1,0:T(8,128)S(1)} %copy-done.3, f32[1,512]{1,0:T(1,128)S(1)} %bitcast.14, f32[4096,512]{1,0:T(8,128)S(1)} %bitcast.11), custom_call_target="tpu_custom_call" | custom-call | tf_op jit(solution)/shard_map/backward_map/pallas_call | solution.py:187
  79.7 0.1 collective-permute-start.3
  79.8 1.2 %collective-permute-done.3 = f32[2,64,128]{2,1,0:T(8,128)S(1)} collective-permute-done((f32[2,64,128]{2,1,0:T(8,128)S(1)}, f32[2,64,128]{2,1,0:T(8,128)S(1)}, u32[]{:S(2)}, u32[]{:S(2)}) %collective-permute-start.3) | collective-permute-done | bytes 65568 | tf_op jit(solution)/shard_map/ppermute | solution.py:201
  81.0 3.0 %collective-permute-start.4 = (f32[64,128]{1,0:T(8,128)S(1)}, f32[64,128]{1,0:T(8,128)S(1)}, u32[]{:S(2)}, u32[]{:S(2)}) collective-permute-start(f32[64,128]{1,0:T(8,128)S(1)} %slice_bitcast_fusion), channel_id=1, source_target_pairs={{0,64},{32,96},{64,0},{96,32},{1,65},{33,97},{65,1},{97,33},{2,66}... | collective-permute-start | bytes 98312 | tf_op jit(solution)/shard_map/ppermute | solution.py:202
  84.0 2.5 %collective-permute-done.4 = f32[64,128]{1,0:T(8,128)S(1)} collective-permute-done((f32[64,128]{1,0:T(8,128)S(1)}, f32[64,128]{1,0:T(8,128)S(1)}, u32[]{:S(2)}, u32[]{:S(2)}) %collective-permute-start.4) | collective-permute-done | bytes 32800 | tf_op jit(solution)/shard_map/ppermute | solution.py:202
  86.5 0.6 fusion
  (5 shorter events, 0.0 us)
Async XLA Ops:
  0.0 5.6 %collective-permute-start.1 = (f32[64,128]{1,0:T(8,128)}, f32[64,128]{1,0:T(8,128)S(1)}, u32[]{:S(2)}, u32[]{:S(2)}) collective-permute-start(f32[64,128]{1,0:T(8,128)} %p0.1), channel_id=1, source_target_pairs={{0,64},{32,96},{64,0},{96,32},{1,65},{33,97},{65,1},{97,33},{2,66}... | collective-permute-start | bytes 98312 | tf_op jit(solution)/shard_map/ppermute | solution.py:159
  3.3 2.4 %collective-permute-start = (f32[64,128]{1,0:T(8,128)}, f32[64,128]{1,0:T(8,128)S(1)}, u32[]{:S(2)}, u32[]{:S(2)}) collective-permute-start(f32[64,128]{1,0:T(8,128)} %p0.1), channel_id=1, source_target_pairs={{0,32},{32,0},{64,96},{96,64},{1,33},{33,1},{65,97},{97,65},{2,34}... | collective-permute-start | bytes 98312 | tf_op jit(solution)/shard_map/ppermute | solution.py:160
  5.6 1.2 %collective-permute-start.2 = (f32[64,128]{1,0:T(8,128)S(1)}, f32[64,128]{1,0:T(8,128)S(1)}, u32[]{:S(2)}, u32[]{:S(2)}) collective-permute-start(f32[64,128]{1,0:T(8,128)S(1)} %collective-permute-done.1.p2), channel_id=1, source_target_pairs={{0,32},{32,0},{64,96},{96,64},{1,33},{33,1},{65,97},{97,65},{2,34}... | collective-permute-start | bytes 98312 | tf_op jit(solution)/shard_map/ppermute | solution.py:161
  6.8 3.4 %copy-start = (f32[64,64,512]{2,1,0:T(8,128)S(1)}, f32[64,64,512]{2,1,0:T(8,128)}, u32[]{:S(2)}) copy-start(f32[64,64,512]{2,1,0:T(8,128)} %param.5) | copy-start | bytes 25165828
  10.2 0.8 copy-start.2
  11.0 55.3 %copy-start.3 = (f32[64,64]{1,0:T(8,128)S(1)}, f32[64,64]{1,0:T(8,128)}, u32[]{:S(2)}) copy-start(f32[64,64]{1,0:T(8,128)} %noise.1) | copy-start | bytes 49156
  11.0 55.3 %copy-start.4 = (f32[512]{0:T(512)S(1)}, f32[512]{0:T(512)}, u32[]{:S(2)}) copy-start(f32[512]{0:T(512)} %param.7) | copy-start | bytes 6148
  66.3 3.4 %copy-start.1 = (f32[64,64,512]{2,1,0:T(8,128)S(1)}, f32[64,64,512]{2,1,0:T(8,128)}, u32[]{:S(2)}) copy-start(f32[64,64,512]{2,1,0:T(8,128)} %param.5) | copy-start | bytes 25165828
  79.7 1.3 %collective-permute-start.3 = (f32[2,64,128]{2,1,0:T(8,128)S(1)}, f32[2,64,128]{2,1,0:T(8,128)S(1)}, u32[]{:S(2)}, u32[]{:S(2)}) collective-permute-start(f32[2,64,128]{2,1,0:T(8,128)S(1)} %get-tuple-element.8), channel_id=1, source_target_pairs={{0,32},{32,0},{64,96},{96,64},{1,33},{33,1},{65,97},{97,65},{2,34}... | collective-permute-start | bytes 196616 | tf_op jit(solution)/shard_map/ppermute | solution.py:201
  81.0 5.5 %collective-permute-start.4 = (f32[64,128]{1,0:T(8,128)S(1)}, f32[64,128]{1,0:T(8,128)S(1)}, u32[]{:S(2)}, u32[]{:S(2)}) collective-permute-start(f32[64,128]{1,0:T(8,128)S(1)} %slice_bitcast_fusion), channel_id=1, source_target_pairs={{0,64},{32,96},{64,0},{96,32},{1,65},{33,97},{65,1},{97,33},{2,66}... | collective-permute-start | bytes 98312 | tf_op jit(solution)/shard_map/ppermute | solution.py:202

commit v2 on v1

v2 whole, which is shorter than its diff:
```python
import jax
import jax.numpy as jnp
from jax import lax
from jax.experimental import pallas as pl
from jax.experimental.pallas import tpu as pltpu
from jax.sharding import PartitionSpec as P

F32 = jnp.float32
BF16 = jnp.bfloat16
GROUP = 4


def split(value):
    high = value.astype(BF16)
    return high, (value - high.astype(F32)).astype(BF16)


def prepare_kernel(kernel_ref, k_high, k_low, held, sems):
    blocks = sems.shape[0]
    block_rows = held.shape[0] // blocks

    def block_copy(b):
        rows = pl.ds(pl.multiple_of(b * block_rows, block_rows), block_rows)
        return rows, pltpu.make_async_copy(kernel_ref.at[rows], held.at[rows], sems.at[b])

    for b in range(blocks):
        block_copy(b)[1].start()

    @pl.loop(0, blocks)
    def _(b):
        rows, copy = block_copy(b)
        copy.wait()
        high, low = split(held[rows, :])
        k_high[rows, :] = high
        k_low[rows, :] = low


def widen_noise(noise, wide_refs):
    time_steps = noise.shape[0]
    columns = wide_refs[0].shape[0]
    row = lax.broadcasted_iota(jnp.int32, (time_steps, columns), 0)
    col = lax.broadcasted_iota(jnp.int32, (time_steps, columns), 1)
    expand = jnp.where(row == col // 8, 1.0, 0.0).astype(BF16)
    same = (
        lax.broadcasted_iota(jnp.int32, (1, 8, columns), 1)
        == lax.broadcasted_iota(jnp.int32, (1, 8, columns), 2) % 8
    )
    for part, wide_ref in zip(split(noise[...]), wide_refs):
        wide = jnp.dot(part, expand, preferred_element_type=F32)
        wide = jnp.where(same, wide[:, None, :], 0.0)
        wide_ref[...] = wide.reshape(columns, columns).astype(BF16)


def forward_kernel(
    p0, p1, p2, p3, noise, k_high, k_low, out_ref, n_high, n_low, field, f_high, f_low
):
    params, part_columns = p0.shape
    columns = out_ref.shape[0]
    block_rows = GROUP * params
    step_rows = 8 * GROUP
    me = lax.axis_index("sens")
    field[pl.ds(0, step_rows), :] = jnp.zeros((step_rows, params), F32)
    for other, piece in enumerate((p0, p1, p2, p3)):
        start = step_rows + part_columns * jnp.bitwise_xor(me, other)
        field[pl.ds(pl.multiple_of(start, step_rows), part_columns), :] = piece[...].T
    shifted = jnp.concatenate(
        [field[pl.ds(step_rows - 8 * lag, columns), :] for lag in range(GROUP)], axis=1
    )
    f_high[...], f_low[...] = split(shifted)
    widen_noise(noise, (n_high, n_low))
    for b in range(k_high.shape[0] // block_rows):
        rows = pl.ds(b * block_rows, block_rows)
        source = pl.ds(0, columns - step_rows * b)
        target = pl.ds(step_rows * b, columns - step_rows * b)
        term = jnp.dot(f_high[source, :], k_high[rows, :], preferred_element_type=F32)
        term += jnp.dot(f_high[source, :], k_low[rows, :], preferred_element_type=F32)
        term += jnp.dot(f_low[source, :], k_high[rows, :], preferred_element_type=F32)
        if b == 0:
            out_ref[target, :] = term
        else:
            out_ref[target, :] += term


def share_kernel(pieces, k_high, k_low, out_ref):
    del k_high, k_low
    total = jnp.sum(pieces[...], axis=0)
    for part in range(out_ref.shape[0]):
        out_ref[part] = total


def backward_kernel(
    observed, n_high, n_low, sensor_weight, k_high, k_low, kept, sent, spread, weighted
):
    columns, sensors = observed.shape
    params = kept.shape[1]
    part_columns = kept.shape[2]
    block_rows = GROUP * params
    step_rows = 8 * GROUP
    o_high, o_low = split(observed[...])
    mixed = jnp.dot(n_high[...], o_high, preferred_element_type=F32)
    mixed += jnp.dot(n_high[...], o_low, preferred_element_type=F32)
    mixed += jnp.dot(n_low[...], o_high, preferred_element_type=F32)
    high, low = split(mixed * sensor_weight[...])
    weighted[:, pl.ds(0, sensors)] = high
    weighted[:, pl.ds(sensors, sensors)] = high
    weighted[:, pl.ds(2 * sensors, sensors)] = low
    spread[pl.ds(columns, step_rows), :] = jnp.zeros((step_rows, block_rows), F32)
    for b in range(k_high.shape[0] // block_rows):
        rows = pl.ds(b * block_rows, block_rows)
        source = pl.ds(step_rows * b, columns - step_rows * b)
        target = pl.ds(0, columns - step_rows * b)
        weights = jnp.concatenate([k_high[rows, :], k_low[rows, :], k_high[rows, :]], axis=1)
        term = lax.dot_general(
            weighted[source, :], weights, (((1,), (1,)), ((), ())), preferred_element_type=F32
        )
        if b == 0:
            spread[target, :] = term
        else:
            spread[target, :] += term

    me = lax.axis_index("sens")
    for other, target in enumerate((kept.at[0], sent.at[0], kept.at[1], sent.at[1])):
        start = pl.multiple_of(part_columns * jnp.bitwise_xor(me, other), part_columns)
        total = spread[pl.ds(start, part_columns), pl.ds(0, params)]
        for lag in range(1, GROUP):
            total += spread[pl.ds(start + 8 * lag, part_columns), pl.ds(lag * params, params)]
        target[...] = total.T


def per_device(probes, kernel, noise_inverse, sensor_weight):
    time_steps, params, sensors = kernel.shape
    part_columns = probes.shape[1]
    ranks = lax.axis_size("sens")
    columns = part_columns * ranks
    blocks = time_steps // GROUP
    block_rows = GROUP * params
    par = lax.axis_size("par")
    swap_core = [(s, s ^ 1) for s in range(ranks)]
    swap_chip = [(s, s ^ 2) for s in range(ranks)]
    kernel_rows = time_steps * params
    vmem = pl.BlockSpec(memory_space=pltpu.VMEM)
    hbm = pl.BlockSpec(memory_space=pltpu.HBM)
    compiler_params = pltpu.CompilerParams(vmem_limit_bytes=24 * 1024 * 1024)
    step_rows = 8 * GROUP

    across = lax.ppermute(probes, "sens", swap_chip)
    diagonal = lax.ppermute(probes, "sens", [(s, s ^ 3) for s in range(ranks)])
    beside = lax.ppermute(probes, "sens", swap_core)

    half_kernel = jax.ShapeDtypeStruct((kernel_rows, sensors), BF16)
    half_noise = jax.ShapeDtypeStruct((columns, columns), BF16)
    k_high, k_low = pl.pallas_call(
        prepare_kernel,
        out_shape=(half_kernel, half_kernel),
        in_specs=[hbm],
        out_specs=(vmem, vmem),
        scratch_shapes=[
            pltpu.VMEM((kernel_rows, sensors), F32),
            pltpu.SemaphoreType.DMA((blocks,)),
        ],
        compiler_params=pltpu.CompilerParams(vmem_limit_bytes=40 * 1024 * 1024),
        cost_estimate=pl.CostEstimate(
            flops=8 * kernel_rows * sensors,
            bytes_accessed=8 * kernel_rows * sensors,
            transcendentals=0,
        ),
        name="prepare",
    )(kernel.reshape(kernel_rows, sensors))

    partial, n_high, n_low = pl.pallas_call(
        forward_kernel,
        out_shape=(
            jax.ShapeDtypeStruct((columns, sensors), F32),
            half_noise,
            half_noise,
        ),
        in_specs=[vmem] * 7,
        out_specs=(vmem,) * 3,
        scratch_shapes=[
            pltpu.VMEM((step_rows + columns, params), F32),
            pltpu.VMEM((columns, block_rows), BF16),
            pltpu.VMEM((columns, block_rows), BF16),
        ],
        compiler_params=compiler_params,
        name="forward_map",
    )(probes, beside, across, diagonal, noise_inverse, k_high, k_low)

    pieces = lax.all_to_all(
        partial.reshape(par, columns // par, sensors), "par", 0, 0, tiled=True
    )
    shares = pl.pallas_call(
        share_kernel,
        out_shape=jax.ShapeDtypeStruct(pieces.shape, F32),
        in_specs=[vmem] * 3,
        out_specs=vmem,
        compiler_params=compiler_params,
        name="share",
    )(pieces, k_high, k_low)
    observed = lax.all_to_all(shares, "par", 0, 0, tiled=True).reshape(columns, sensors)

    piece = jax.ShapeDtypeStruct((2, params, part_columns), F32)
    kept, sent = pl.pallas_call(
        backward_kernel,
        out_shape=(piece, piece),
        in_specs=[vmem] * 6,
        out_specs=(vmem, vmem),
        scratch_shapes=[
            pltpu.VMEM((columns + step_rows, block_rows), F32),
            pltpu.VMEM((columns, 3 * sensors), BF16),
        ],
        compiler_params=compiler_params,
        name="backward_map",
    )(observed, n_high, n_low, sensor_weight.reshape(1, sensors), k_high, k_low)
    kept += lax.ppermute(sent, "sens", swap_core)
    return kept[0] + lax.ppermute(kept[1], "sens", swap_chip)


def solution(mesh):
    placed = (P("par", "sens"), P(None, "par", "sens"), P(), P("sens"))
    return jax.shard_map(
        per_device, mesh=mesh, in_specs=placed, out_specs=P("par", "sens"), check_vma=False
    )
```

time: 87.5 us -> 73.8 us (0.84)
  local copies, waits for them, and re-layouts: 7.65 us -> 0.02 us
  Pallas kernels: 17.9 us -> 14.9 us
  waiting for transfers between devices: 7.31 us -> 5.26 us
    unnamed x10 -> x6, local copies, waits for them, and re-layouts: 7.53 us -> 0.01 us
    pallas_call x1, Pallas kernels: 9.98 us -> 7.06 us  [per_device(): pl.pallas_call(backward_kernel, out_shape=(piece, piece), in_specs=[vmem]...]
    ppermute x1, waiting for transfers between devices: 2.35 us -> 0.01 us  [per_device(): across = lax.ppermute(probes, 'sens', swap_chip)]
    pallas_call x1 -> x3, Pallas kernels: 7.89 us -> 7.83 us  [the longest x1 4.09 us: per_device(): pl.pallas_call(forward_kernel, out_shape=(jax.ShapeDtypeStruct((columns,...]
  transfers between devices with their start and end apart: 5 -> 5, of which waited for: 4 -> 3; matrix products, arithmetic and copies ran while one was open for 0% -> 0% of each run, Pallas kernels for 0% -> 5%
where the time goes in v2:
time: 73.8 us; the launch traced here: 73.6 us
  blocking collectives  46.5 us (63%)
  Pallas kernels  14.9 us (20%)
  starting transfers between devices  6.26 us (8%)
  waiting for transfers between devices  5.26 us (7%)
    all_to_all x1, blocking collectives, per_device(): lax.all_to_all(partial.reshape(par, columns // par, sensors), 'par', 0, 0...  25.6 us
    all_to_all x1, blocking collectives, per_device(): lax.all_to_all(shares, 'par', 0, 0, tiled=True).reshape(columns, sensors)  20.9 us
    pallas_call x1, Pallas kernels, per_device(): pl.pallas_call(backward_kernel, out_shape=(piece, piece), in_specs=[vmem]...  7.06 us
    pallas_call x1, Pallas kernels, per_device(): pl.pallas_call(forward_kernel, out_shape=(jax.ShapeDtypeStruct((columns,...  4.09 us
    pallas_call x1, Pallas kernels, per_device(): pl.pallas_call(prepare_kernel, out_shape=(half_kernel, half_kernel), in_s...  3.6 us
    ppermute x1, starting transfers between devices, per_device(): across = lax.ppermute(probes, 'sens', swap_chip)  3.28 us
    ppermute x1, waiting for transfers between devices, per_device(): return kept[0] + lax.ppermute(kept[1], 'sens', swap_chip)  2.96 us
    ppermute x1, starting transfers between devices, per_device(): return kept[0] + lax.ppermute(kept[1], 'sens', swap_chip)  2.53 us
  transfers between devices with their start and end apart: 5, of which 3 were waited for; matrix products, arithmetic and copies ran while one was open for 0% of the time, Pallas kernels for 5%

profile of v2, /device:TPU:0, one launch (start us, length us, event | category | flops | bytes accessed | tf_op | source)
XLA Modules:
  0.0 73.6 jit_solution(10876008977376931689)
XLA Ops:
  0.0 3.3 %collective-permute-start.1 = (f32[64,128]{1,0:T(8,128)}, f32[64,128]{1,0:T(8,128)S(1)}, u32[]{:S(2)}, u32[]{:S(2)}) collective-permute-start(f32[64,128]{1,0:T(8,128)} %p0.1), channel_id=1, source_target_pairs={{0,64},{32,96},{64,0},{96,32},{1,65},{33,97},{65,1},{97,33},{2,66}... | collective-permute-start | bytes 98312 | tf_op jit(solution)/shard_map/ppermute | solution.py:146
  3.3 0.0 collective-permute-start
  3.3 0.4 collective-permute-start.2
  3.6 0.0 copy-start
  3.6 0.0 copy-start.1
  3.7 3.6 %prepare.1 = (bf16[4096,512]{1,0:T(8,128)(2,1)S(1)}, bf16[4096,512]{1,0:T(8,128)(2,1)S(1)}) custom-call(f32[4096,512]{1,0:T(8,128)} %bitcast.13), custom_call_target="tpu_custom_call" | custom-call | flops 16777216 | bytes 16777216 | tf_op jit(solution)/shard_map/prepare/pallas_call | solution.py:152
  7.3 0.0 collective-permute-done.1.p2
  7.3 0.0 collective-permute-done.p1
  7.3 1.1 %collective-permute-done.2.p3 = f32[64,128]{1,0:T(8,128)S(1)} collective-permute-done((f32[64,128]{1,0:T(8,128)}, f32[64,128]{1,0:T(8,128)S(1)}, u32[]{:S(2)}, u32[]{:S(2)}) %collective-permute-start.2) | collective-permute-done | bytes 32800 | tf_op jit(solution)/shard_map/ppermute | solution.py:147
  8.3 0.0 copy-done
  8.3 0.0 copy-done.1
  8.3 4.1 %forward_map.1 = (f32[512,512]{1,0:T(8,128)S(1)}, bf16[512,512]{1,0:T(8,128)(2,1)S(1)}, bf16[512,512]{1,0:T(8,128)(2,1)S(1)}) custom-call(f32[64,128]{1,0:T(8,128)S(1)} %copy-done, f32[64,128]{1,0:T(8,128)S(1)} %collective-permute-done.p1, f32[64,128]{1,0:T(8,128)S(1)} %collective-permute-done.1.p2, f32[64,128]{1,0:T(8,128)S(1)} %collective-permute-done.2.p3, ...), custom_call_target="tpu_custom_call" | custom-call | tf_op jit(solution)/shard_map/forward_map/pallas_call | solution.py:170
  12.4 25.6 %all_to_all.10.pieces = f32[32,16,512]{2,1,0:T(8,128)S(1)} all-to-all(f32[32,16,512]{2,1,0:T(8,128)S(1)} %bitcast.11), channel_id=1, replica_groups=mesh['sens'=4,'par'=32] {'par'}, dimensions={0} | all-to-all | bytes 2097152 | tf_op jit(solution)/shard_map/all_to_all | solution.py:188
  38.1 0.0 copy-start.2
  38.1 0.1 share.1
  38.2 20.9 %all_to_all.11 = f32[32,16,512]{2,1,0:T(8,128)S(1)} all-to-all(f32[32,16,512]{2,1,0:T(8,128)S(1)} %share.1), channel_id=1, replica_groups=mesh['sens'=4,'par'=32] {'par'}, dimensions={0} | all-to-all | bytes 2097152 | tf_op jit(solution)/shard_map/all_to_all | solution.py:199
  59.1 0.0 copy-done.2
  59.1 7.1 %backward_map.1 = (f32[2,64,128]{2,1,0:T(8,128)S(1)}, f32[2,64,128]{2,1,0:T(8,128)S(1)}) custom-call(f32[512,512]{1,0:T(8,128)S(1)} %bitcast.10, bf16[512,512]{1,0:T(8,128)(2,1)S(1)} %get-tuple-element.15.n_high, bf16[512,512]{1,0:T(8,128)(2,1)S(1)} %get-tuple-element.16.n_low, f32[1,512]{1,0:T(1,128)S(1)} %bitcast.12, ...), custom_call_target="tpu_custom_call" | custom-call | tf_op jit(solution)/shard_map/backward_map/pallas_call | solution.py:202
  66.1 0.1 collective-permute-start.3
  66.2 1.2 %collective-permute-done.3 = f32[2,64,128]{2,1,0:T(8,128)S(1)} collective-permute-done((f32[2,64,128]{2,1,0:T(8,128)S(1)}, f32[2,64,128]{2,1,0:T(8,128)S(1)}, u32[]{:S(2)}, u32[]{:S(2)}) %collective-permute-start.3) | collective-permute-done | bytes 65568 | tf_op jit(solution)/shard_map/ppermute | solution.py:214
  67.5 2.5 %collective-permute-start.4 = (f32[64,128]{1,0:T(8,128)S(1)}, f32[64,128]{1,0:T(8,128)S(1)}, u32[]{:S(2)}, u32[]{:S(2)}) collective-permute-start(f32[64,128]{1,0:T(8,128)S(1)} %slice_bitcast_fusion), channel_id=1, source_target_pairs={{0,64},{32,96},{64,0},{96,32},{1,65},{33,97},{65,1},{97,33},{2,66}... | collective-permute-start | bytes 98312 | tf_op jit(solution)/shard_map/ppermute | solution.py:215
  70.0 3.0 %collective-permute-done.4 = f32[64,128]{1,0:T(8,128)S(1)} collective-permute-done((f32[64,128]{1,0:T(8,128)S(1)}, f32[64,128]{1,0:T(8,128)S(1)}, u32[]{:S(2)}, u32[]{:S(2)}) %collective-permute-start.4) | collective-permute-done | bytes 32800 | tf_op jit(solution)/shard_map/ppermute | solution.py:215
  73.0 0.6 fusion
  (2 shorter events, 0.0 us)
Async XLA Ops:
  0.0 7.3 %collective-permute-start.1 = (f32[64,128]{1,0:T(8,128)}, f32[64,128]{1,0:T(8,128)S(1)}, u32[]{:S(2)}, u32[]{:S(2)}) collective-permute-start(f32[64,128]{1,0:T(8,128)} %p0.1), channel_id=1, source_target_pairs={{0,64},{32,96},{64,0},{96,32},{1,65},{33,97},{65,1},{97,33},{2,66}... | collective-permute-start | bytes 98312 | tf_op jit(solution)/shard_map/ppermute | solution.py:146
  3.3 4.0 %collective-permute-start = (f32[64,128]{1,0:T(8,128)}, f32[64,128]{1,0:T(8,128)S(1)}, u32[]{:S(2)}, u32[]{:S(2)}) collective-permute-start(f32[64,128]{1,0:T(8,128)} %p0.1), channel_id=1, source_target_pairs={{0,32},{32,0},{64,96},{96,64},{1,33},{33,1},{65,97},{97,65},{2,34}... | collective-permute-start | bytes 98312 | tf_op jit(solution)/shard_map/ppermute | solution.py:148
  3.3 5.1 %collective-permute-start.2 = (f32[64,128]{1,0:T(8,128)}, f32[64,128]{1,0:T(8,128)S(1)}, u32[]{:S(2)}, u32[]{:S(2)}) collective-permute-start(f32[64,128]{1,0:T(8,128)} %p0.1), channel_id=1, source_target_pairs={{0,96},{32,64},{64,32},{96,0},{1,97},{33,65},{65,33},{97,1},{2,98}... | collective-permute-start | bytes 98312 | tf_op jit(solution)/shard_map/ppermute | solution.py:147
  3.6 4.7 %copy-start = (f32[64,128]{1,0:T(8,128)S(1)}, f32[64,128]{1,0:T(8,128)}, u32[]{:S(2)}) copy-start(f32[64,128]{1,0:T(8,128)} %p0.1) | copy-start | bytes 98308
  3.6 4.7 %copy-start.1 = (f32[64,64]{1,0:T(8,128)S(1)}, f32[64,64]{1,0:T(8,128)}, u32[]{:S(2)}) copy-start(f32[64,64]{1,0:T(8,128)} %noise.1) | copy-start | bytes 49156
  38.1 21.0 %copy-start.2 = (f32[512]{0:T(512)S(1)}, f32[512]{0:T(512)}, u32[]{:S(2)}) copy-start(f32[512]{0:T(512)} %param.7) | copy-start | bytes 6148
  66.1 1.3 %collective-permute-start.3 = (f32[2,64,128]{2,1,0:T(8,128)S(1)}, f32[2,64,128]{2,1,0:T(8,128)S(1)}, u32[]{:S(2)}, u32[]{:S(2)}) collective-permute-start(f32[2,64,128]{2,1,0:T(8,128)S(1)} %get-tuple-element.18), channel_id=1, source_target_pairs={{0,32},{32,0},{64,96},{96,64},{1,33},{33,1},{65,97},{97,65},{2,34}... | collective-permute-start | bytes 196616 | tf_op jit(solution)/shard_map/ppermute | solution.py:214
  67.5 5.5 %collective-permute-start.4 = (f32[64,128]{1,0:T(8,128)S(1)}, f32[64,128]{1,0:T(8,128)S(1)}, u32[]{:S(2)}, u32[]{:S(2)}) collective-permute-start(f32[64,128]{1,0:T(8,128)S(1)} %slice_bitcast_fusion), channel_id=1, source_target_pairs={{0,64},{32,96},{64,0},{96,32},{1,65},{33,97},{65,1},{97,33},{2,66}... | collective-permute-start | bytes 98312 | tf_op jit(solution)/shard_map/ppermute | solution.py:215

commit v3 on v2

--- a/solution.py
+++ b/solution.py
@@ -8,11 +8,16 @@
 F32 = jnp.float32
 BF16 = jnp.bfloat16
 GROUP = 4
+NOISE_ROWS = 128
 
 
 def split(value):
     high = value.astype(BF16)
     return high, (value - high.astype(F32)).astype(BF16)
+
+
+def transposed_dot(left, right):
+    return lax.dot_general(left, right, (((1,), (1,)), ((), ())), preferred_element_type=F32)
 
 
 def prepare_kernel(kernel_ref, k_high, k_low, held, sems):
@@ -89,30 +94,29 @@
 
 
 def backward_kernel(
-    observed, n_high, n_low, sensor_weight, k_high, k_low, kept, sent, spread, weighted
+    observed, n_high, n_low, sensor_weight, k_high, k_low, kept, sent,
+    spread, w_high, w_low, o_high, o_low,
 ):
     columns, sensors = observed.shape
     params = kept.shape[1]
     part_columns = kept.shape[2]
     block_rows = GROUP * params
     step_rows = 8 * GROUP
-    o_high, o_low = split(observed[...])
-    mixed = jnp.dot(n_high[...], o_high, preferred_element_type=F32)
-    mixed += jnp.dot(n_high[...], o_low, preferred_element_type=F32)
-    mixed += jnp.dot(n_low[...], o_high, preferred_element_type=F32)
-    high, low = split(mixed * sensor_weight[...])
-    weighted[:, pl.ds(0, sensors)] = high
-    weighted[:, pl.ds(sensors, sensors)] = high
-    weighted[:, pl.ds(2 * sensors, sensors)] = low
+    o_high[...], o_low[...] = split(observed[...])
+    for start in range(0, columns, NOISE_ROWS):
+        rows = pl.ds(start, NOISE_ROWS)
+        mixed = jnp.dot(n_high[rows, :], o_high[...], preferred_element_type=F32)
+        mixed += jnp.dot(n_high[rows, :], o_low[...], preferred_element_type=F32)
+        mixed += jnp.dot(n_low[rows, :], o_high[...], preferred_element_type=F32)
+        w_high[rows, :], w_low[rows, :] = split(mixed * sensor_weight[...])
     spread[pl.ds(columns, step_rows), :] = jnp.zeros((step_rows, block_rows), F32)
     for b in range(k_high.shape[0] // block_rows):
         rows = pl.ds(b * block_rows, block_rows)
         source = pl.ds(step_rows * b, columns - step_rows * b)
         target = pl.ds(0, columns - step_rows * b)
-        weights = jnp.concatenate([k_high[rows, :], k_low[rows, :], k_high[rows, :]], axis=1)
-        term = lax.dot_general(
-            weighted[source, :], weights, (((1,), (1,)), ((), ())), preferred_element_type=F32
-        )
+        term = transposed_dot(w_high[source, :], k_high[rows, :])
+        term += transposed_dot(w_high[source, :], k_low[rows, :])
+        term += transposed_dot(w_low[source, :], k_high[rows, :])
         if b == 0:
             spread[target, :] = term
         else:
@@ -206,7 +210,10 @@
         out_specs=(vmem, vmem),
         scratch_shapes=[
             pltpu.VMEM((columns + step_rows, block_rows), F32),
-            pltpu.VMEM((columns, 3 * sensors), BF16),
+            pltpu.VMEM((columns, sensors), BF16),
+            pltpu.VMEM((columns, sensors), BF16),
+            pltpu.VMEM((columns, sensors), BF16),
+            pltpu.VMEM((columns, sensors), BF16),
         ],
         compiler_params=compiler_params,
         name="backward_map",

time: 73.8 us -> 72.3 us (0.980)
  Pallas kernels: 14.9 us -> 13.4 us
    pallas_call x1, Pallas kernels: 7.06 us -> 5.59 us  [per_device(): pl.pallas_call(backward_kernel, out_shape=(piece, piece), in_specs=[vmem]...]
where the time goes in v3:
time: 72.3 us; the launch traced here: 72.1 us
  blocking collectives  46.5 us (64%)
  Pallas kernels  13.4 us (19%)
  starting transfers between devices  6.29 us (9%)
  waiting for transfers between devices  5.24 us (7%)
    all_to_all x1, blocking collectives, per_device(): lax.all_to_all(partial.reshape(par, columns // par, sensors), 'par', 0, 0...  25.6 us
    all_to_all x1, blocking collectives, per_device(): lax.all_to_all(shares, 'par', 0, 0, tiled=True).reshape(columns, sensors)  20.9 us
    pallas_call x1, Pallas kernels, per_device(): pl.pallas_call(backward_kernel, out_shape=(piece, piece), in_specs=[vmem]...  5.59 us
    pallas_call x1, Pallas kernels, per_device(): pl.pallas_call(forward_kernel, out_shape=(jax.ShapeDtypeStruct((columns,...  4.09 us
    pallas_call x1, Pallas kernels, per_device(): pl.pallas_call(prepare_kernel, out_shape=(half_kernel, half_kernel), in_s...  3.6 us
    ppermute x1, starting transfers between devices, per_device(): across = lax.ppermute(probes, 'sens', swap_chip)  3.28 us
    ppermute x1, waiting for transfers between devices, per_device(): return kept[0] + lax.ppermute(kept[1], 'sens', swap_chip)  2.94 us
    ppermute x1, starting transfers between devices, per_device(): return kept[0] + lax.ppermute(kept[1], 'sens', swap_chip)  2.56 us
  transfers between devices with their start and end apart: 5, of which 3 were waited for; matrix products, arithmetic and copies ran while one was open for 0% of the time, Pallas kernels for 5%

profile of v3, /device:TPU:0, one launch (start us, length us, event | category | flops | bytes accessed | tf_op | source)
XLA Modules:
  0.0 72.1 jit_solution(13134565638665444297)
XLA Ops:
  0.0 3.3 %collective-permute-start.1 = (f32[64,128]{1,0:T(8,128)}, f32[64,128]{1,0:T(8,128)S(1)}, u32[]{:S(2)}, u32[]{:S(2)}) collective-permute-start(f32[64,128]{1,0:T(8,128)} %p0.1), channel_id=1, source_target_pairs={{0,64},{32,96},{64,0},{96,32},{1,65},{33,97},{65,1},{97,33},{2,66}... | collective-permute-start | bytes 98312 | tf_op jit(solution)/shard_map/ppermute | solution.py:150
  3.3 0.0 collective-permute-start
  3.3 0.4 collective-permute-start.2
  3.6 0.0 copy-start
  3.6 0.0 copy-start.1
  3.7 3.6 %prepare.1 = (bf16[4096,512]{1,0:T(8,128)(2,1)S(1)}, bf16[4096,512]{1,0:T(8,128)(2,1)S(1)}) custom-call(f32[4096,512]{1,0:T(8,128)} %bitcast.13), custom_call_target="tpu_custom_call" | custom-call | flops 16777216 | bytes 16777216 | tf_op jit(solution)/shard_map/prepare/pallas_call | solution.py:156
  7.3 0.0 collective-permute-done.1.p2
  7.3 0.0 collective-permute-done.p1
  7.3 1.1 %collective-permute-done.2.p3 = f32[64,128]{1,0:T(8,128)S(1)} collective-permute-done((f32[64,128]{1,0:T(8,128)}, f32[64,128]{1,0:T(8,128)S(1)}, u32[]{:S(2)}, u32[]{:S(2)}) %collective-permute-start.2) | collective-permute-done | bytes 32800 | tf_op jit(solution)/shard_map/ppermute | solution.py:151
  8.3 0.0 copy-done
  8.3 0.0 copy-done.1
  8.3 4.1 %forward_map.1 = (f32[512,512]{1,0:T(8,128)S(1)}, bf16[512,512]{1,0:T(8,128)(2,1)S(1)}, bf16[512,512]{1,0:T(8,128)(2,1)S(1)}) custom-call(f32[64,128]{1,0:T(8,128)S(1)} %copy-done, f32[64,128]{1,0:T(8,128)S(1)} %collective-permute-done.p1, f32[64,128]{1,0:T(8,128)S(1)} %collective-permute-done.1.p2, f32[64,128]{1,0:T(8,128)S(1)} %collective-permute-done.2.p3, ...), custom_call_target="tpu_custom_call" | custom-call | tf_op jit(solution)/shard_map/forward_map/pallas_call | solution.py:174
  12.4 25.6 %all_to_all.10.pieces = f32[32,16,512]{2,1,0:T(8,128)S(1)} all-to-all(f32[32,16,512]{2,1,0:T(8,128)S(1)} %bitcast.11), channel_id=1, replica_groups=mesh['sens'=4,'par'=32] {'par'}, dimensions={0} | all-to-all | bytes 2097152 | tf_op jit(solution)/shard_map/all_to_all | solution.py:192
  38.1 0.0 copy-start.2
  38.1 0.1 share.1
  38.2 20.9 %all_to_all.11 = f32[32,16,512]{2,1,0:T(8,128)S(1)} all-to-all(f32[32,16,512]{2,1,0:T(8,128)S(1)} %share.1), channel_id=1, replica_groups=mesh['sens'=4,'par'=32] {'par'}, dimensions={0} | all-to-all | bytes 2097152 | tf_op jit(solution)/shard_map/all_to_all | solution.py:203
  59.1 0.0 copy-done.2
  59.1 5.6 %backward_map.1 = (f32[2,64,128]{2,1,0:T(8,128)S(1)}, f32[2,64,128]{2,1,0:T(8,128)S(1)}) custom-call(f32[512,512]{1,0:T(8,128)S(1)} %bitcast.10, bf16[512,512]{1,0:T(8,128)(2,1)S(1)} %get-tuple-element.15.n_high, bf16[512,512]{1,0:T(8,128)(2,1)S(1)} %get-tuple-element.16.n_low, f32[1,512]{1,0:T(1,128)S(1)} %bitcast.12, ...), custom_call_target="tpu_custom_call" | custom-call | tf_op jit(solution)/shard_map/backward_map/pallas_call | solution.py:206
  64.7 0.1 collective-permute-start.3
  64.8 1.2 %collective-permute-done.3 = f32[2,64,128]{2,1,0:T(8,128)S(1)} collective-permute-done((f32[2,64,128]{2,1,0:T(8,128)S(1)}, f32[2,64,128]{2,1,0:T(8,128)S(1)}, u32[]{:S(2)}, u32[]{:S(2)}) %collective-permute-start.3) | collective-permute-done | bytes 65568 | tf_op jit(solution)/shard_map/ppermute | solution.py:221
  66.0 2.6 %collective-permute-start.4 = (f32[64,128]{1,0:T(8,128)S(1)}, f32[64,128]{1,0:T(8,128)S(1)}, u32[]{:S(2)}, u32[]{:S(2)}) collective-permute-start(f32[64,128]{1,0:T(8,128)S(1)} %slice_bitcast_fusion), channel_id=1, source_target_pairs={{0,64},{32,96},{64,0},{96,32},{1,65},{33,97},{65,1},{97,33},{2,66}... | collective-permute-start | bytes 98312 | tf_op jit(solution)/shard_map/ppermute | solution.py:222
  68.6 2.9 %collective-permute-done.4 = f32[64,128]{1,0:T(8,128)S(1)} collective-permute-done((f32[64,128]{1,0:T(8,128)S(1)}, f32[64,128]{1,0:T(8,128)S(1)}, u32[]{:S(2)}, u32[]{:S(2)}) %collective-permute-start.4) | collective-permute-done | bytes 32800 | tf_op jit(solution)/shard_map/ppermute | solution.py:222
  71.5 0.6 fusion
  (2 shorter events, 0.0 us)
Async XLA Ops:
  0.0 7.3 %collective-permute-start.1 = (f32[64,128]{1,0:T(8,128)}, f32[64,128]{1,0:T(8,128)S(1)}, u32[]{:S(2)}, u32[]{:S(2)}) collective-permute-start(f32[64,128]{1,0:T(8,128)} %p0.1), channel_id=1, source_target_pairs={{0,64},{32,96},{64,0},{96,32},{1,65},{33,97},{65,1},{97,33},{2,66}... | collective-permute-start | bytes 98312 | tf_op jit(solution)/shard_map/ppermute | solution.py:150
  3.3 4.0 %collective-permute-start = (f32[64,128]{1,0:T(8,128)}, f32[64,128]{1,0:T(8,128)S(1)}, u32[]{:S(2)}, u32[]{:S(2)}) collective-permute-start(f32[64,128]{1,0:T(8,128)} %p0.1), channel_id=1, source_target_pairs={{0,32},{32,0},{64,96},{96,64},{1,33},{33,1},{65,97},{97,65},{2,34}... | collective-permute-start | bytes 98312 | tf_op jit(solution)/shard_map/ppermute | solution.py:152
  3.3 5.1 %collective-permute-start.2 = (f32[64,128]{1,0:T(8,128)}, f32[64,128]{1,0:T(8,128)S(1)}, u32[]{:S(2)}, u32[]{:S(2)}) collective-permute-start(f32[64,128]{1,0:T(8,128)} %p0.1), channel_id=1, source_target_pairs={{0,96},{32,64},{64,32},{96,0},{1,97},{33,65},{65,33},{97,1},{2,98}... | collective-permute-start | bytes 98312 | tf_op jit(solution)/shard_map/ppermute | solution.py:151
  3.6 4.7 %copy-start = (f32[64,128]{1,0:T(8,128)S(1)}, f32[64,128]{1,0:T(8,128)}, u32[]{:S(2)}) copy-start(f32[64,128]{1,0:T(8,128)} %p0.1) | copy-start | bytes 98308
  3.6 4.7 %copy-start.1 = (f32[64,64]{1,0:T(8,128)S(1)}, f32[64,64]{1,0:T(8,128)}, u32[]{:S(2)}) copy-start(f32[64,64]{1,0:T(8,128)} %noise.1) | copy-start | bytes 49156
  38.1 21.0 %copy-start.2 = (f32[512]{0:T(512)S(1)}, f32[512]{0:T(512)}, u32[]{:S(2)}) copy-start(f32[512]{0:T(512)} %param.7) | copy-start | bytes 6148
  64.7 1.3 %collective-permute-start.3 = (f32[2,64,128]{2,1,0:T(8,128)S(1)}, f32[2,64,128]{2,1,0:T(8,128)S(1)}, u32[]{:S(2)}, u32[]{:S(2)}) collective-permute-start(f32[2,64,128]{2,1,0:T(8,128)S(1)} %get-tuple-element.18), channel_id=1, source_target_pairs={{0,32},{32,0},{64,96},{96,64},{1,33},{33,1},{65,97},{97,65},{2,34}... | collective-permute-start | bytes 196616 | tf_op jit(solution)/shard_map/ppermute | solution.py:221
  66.0 5.5 %collective-permute-start.4 = (f32[64,128]{1,0:T(8,128)S(1)}, f32[64,128]{1,0:T(8,128)S(1)}, u32[]{:S(2)}, u32[]{:S(2)}) collective-permute-start(f32[64,128]{1,0:T(8,128)S(1)} %slice_bitcast_fusion), channel_id=1, source_target_pairs={{0,64},{32,96},{64,0},{96,32},{1,65},{33,97},{65,1},{97,33},{2,66}... | collective-permute-start | bytes 98312 | tf_op jit(solution)/shard_map/ppermute | solution.py:222

commit v4 on v3

--- a/solution.py
+++ b/solution.py
@@ -8,6 +8,7 @@
 F32 = jnp.float32
 BF16 = jnp.bfloat16
 GROUP = 4
+PIECES = 8
 NOISE_ROWS = 128
 
 
@@ -77,9 +78,10 @@
         rows = pl.ds(b * block_rows, block_rows)
         source = pl.ds(0, columns - step_rows * b)
         target = pl.ds(step_rows * b, columns - step_rows * b)
-        term = jnp.dot(f_high[source, :], k_high[rows, :], preferred_element_type=F32)
+        both = jnp.concatenate([f_high[source, :], f_low[source, :]], axis=0)
+        both = jnp.dot(both, k_high[rows, :], preferred_element_type=F32)
+        term = both[: source.size] + both[source.size :]
         term += jnp.dot(f_high[source, :], k_low[rows, :], preferred_element_type=F32)
-        term += jnp.dot(f_low[source, :], k_high[rows, :], preferred_element_type=F32)
         if b == 0:
             out_ref[target, :] = term
         else:
@@ -114,9 +116,10 @@
         rows = pl.ds(b * block_rows, block_rows)
         source = pl.ds(step_rows * b, columns - step_rows * b)
         target = pl.ds(0, columns - step_rows * b)
-        term = transposed_dot(w_high[source, :], k_high[rows, :])
+        both = jnp.concatenate([w_high[source, :], w_low[source, :]], axis=0)
+        both = transposed_dot(both, k_high[rows, :])
+        term = both[: source.size] + both[source.size :]
         term += transposed_dot(w_high[source, :], k_low[rows, :])
-        term += transposed_dot(w_low[source, :], k_high[rows, :])
         if b == 0:
             spread[target, :] = term
         else:
@@ -136,7 +139,6 @@
     part_columns = probes.shape[1]
     ranks = lax.axis_size("sens")
     columns = part_columns * ranks
-    blocks = time_steps // GROUP
     block_rows = GROUP * params
     par = lax.axis_size("par")
     swap_core = [(s, s ^ 1) for s in range(ranks)]
@@ -148,7 +150,6 @@
     step_rows = 8 * GROUP
 
     across = lax.ppermute(probes, "sens", swap_chip)
-    diagonal = lax.ppermute(probes, "sens", [(s, s ^ 3) for s in range(ranks)])
     beside = lax.ppermute(probes, "sens", swap_core)
 
     half_kernel = jax.ShapeDtypeStruct((kernel_rows, sensors), BF16)
@@ -160,7 +161,7 @@
         out_specs=(vmem, vmem),
         scratch_shapes=[
             pltpu.VMEM((kernel_rows, sensors), F32),
-            pltpu.SemaphoreType.DMA((blocks,)),
+            pltpu.SemaphoreType.DMA((PIECES,)),
         ],
         compiler_params=pltpu.CompilerParams(vmem_limit_bytes=40 * 1024 * 1024),
         cost_estimate=pl.CostEstimate(
@@ -170,6 +171,9 @@
         ),
         name="prepare",
     )(kernel.reshape(kernel_rows, sensors))
+
+    across, k_high = lax.optimization_barrier((across, k_high))
+    diagonal = lax.ppermute(across, "sens", swap_core)
 
     partial, n_high, n_low = pl.pallas_call(
         forward_kernel,

time: 72.3 us -> 71.5 us (0.989)
  no operation moved by 1% of the time
where the time goes in v4:
time: 71.5 us; the launch traced here: 71.3 us
  blocking collectives  46.1 us (64%)
  Pallas kernels  12.9 us (18%)
  starting transfers between devices  6.5 us (9%)
  waiting for transfers between devices  5.05 us (7%)
    all_to_all x1, blocking collectives, per_device(): lax.all_to_all(partial.reshape(par, columns // par, sensors), 'par', 0, 0...  25.5 us
    all_to_all x1, blocking collectives, per_device(): lax.all_to_all(shares, 'par', 0, 0, tiled=True).reshape(columns, sensors)  20.6 us
    pallas_call x1, Pallas kernels, per_device(): pl.pallas_call(backward_kernel, out_shape=(piece, piece), in_specs=[vmem]...  5.25 us
    pallas_call x1, Pallas kernels, per_device(): pl.pallas_call(forward_kernel, out_shape=(jax.ShapeDtypeStruct((columns,...  3.91 us
    pallas_call x1, Pallas kernels, per_device(): pl.pallas_call(prepare_kernel, out_shape=(half_kernel, half_kernel), in_s...  3.61 us
    ppermute x1, starting transfers between devices, per_device(): across = lax.ppermute(probes, 'sens', swap_chip)  3.28 us
    ppermute x1, waiting for transfers between devices, per_device(): return kept[0] + lax.ppermute(kept[1], 'sens', swap_chip)  2.95 us
    ppermute x1, starting transfers between devices, per_device(): return kept[0] + lax.ppermute(kept[1], 'sens', swap_chip)  2.55 us
  transfers between devices with their start and end apart: 5, of which 3 were waited for; matrix products, arithmetic and copies ran while one was open for 0% of the time, Pallas kernels for 5%

profile of v4, /device:TPU:0, one launch (start us, length us, event | category | flops | bytes accessed | tf_op | source)
XLA Modules:
  0.0 71.3 jit_solution(2534102971023634775)
XLA Ops:
  0.0 3.3 %collective-permute-start.1 = (f32[64,128]{1,0:T(8,128)}, f32[64,128]{1,0:T(8,128)S(1)}, u32[]{:S(2)}, u32[]{:S(2)}) collective-permute-start(f32[64,128]{1,0:T(8,128)} %p0.1), channel_id=1, source_target_pairs={{0,64},{32,96},{64,0},{96,32},{1,65},{33,97},{65,1},{97,33},{2,66}... | collective-permute-start | bytes 98312 | tf_op jit(solution)/shard_map/ppermute | solution.py:152
  3.3 0.0 collective-permute-start
  3.3 0.0 copy-start
  3.3 0.0 copy-start.1
  3.3 3.6 %prepare.1 = (bf16[4096,512]{1,0:T(8,128)(2,1)S(1)}, bf16[4096,512]{1,0:T(8,128)(2,1)S(1)}) custom-call(f32[4096,512]{1,0:T(8,128)} %bitcast.13), custom_call_target="tpu_custom_call" | custom-call | flops 16777216 | bytes 16777216 | tf_op jit(solution)/shard_map/prepare/pallas_call | solution.py:157
  6.9 0.0 collective-permute-done.1.p2
  6.9 0.6 collective-permute-start.2
  7.5 0.0 collective-permute-done.p1
  7.5 0.9 %collective-permute-done.2.p3 = f32[64,128]{1,0:T(8,128)S(1)} collective-permute-done((f32[64,128]{1,0:T(8,128)S(1)}, f32[64,128]{1,0:T(8,128)S(1)}, u32[]{:S(2)}, u32[]{:S(2)}) %collective-permute-start.2) | collective-permute-done | bytes 32800 | tf_op jit(solution)/shard_map/ppermute | solution.py:176
  8.4 0.0 copy-done
  8.4 0.0 copy-done.1
  8.4 3.9 %forward_map.1 = (f32[512,512]{1,0:T(8,128)S(1)}, bf16[512,512]{1,0:T(8,128)(2,1)S(1)}, bf16[512,512]{1,0:T(8,128)(2,1)S(1)}) custom-call(f32[64,128]{1,0:T(8,128)S(1)} %copy-done, f32[64,128]{1,0:T(8,128)S(1)} %collective-permute-done.p1, f32[64,128]{1,0:T(8,128)S(1)} %collective-permute-done.1.p2, f32[64,128]{1,0:T(8,128)S(1)} %collective-permute-done.2.p3, ...), custom_call_target="tpu_custom_call" | custom-call | tf_op jit(solution)/shard_map/forward_map/pallas_call | solution.py:178
  12.3 25.5 %all_to_all.10.pieces = f32[32,16,512]{2,1,0:T(8,128)S(1)} all-to-all(f32[32,16,512]{2,1,0:T(8,128)S(1)} %bitcast.11), channel_id=1, replica_groups=mesh['sens'=4,'par'=32] {'par'}, dimensions={0} | all-to-all | bytes 2097152 | tf_op jit(solution)/shard_map/all_to_all | solution.py:196
  37.8 0.0 copy-start.2
  37.8 0.1 share.1
  37.9 20.6 %all_to_all.11 = f32[32,16,512]{2,1,0:T(8,128)S(1)} all-to-all(f32[32,16,512]{2,1,0:T(8,128)S(1)} %share.1), channel_id=1, replica_groups=mesh['sens'=4,'par'=32] {'par'}, dimensions={0} | all-to-all | bytes 2097152 | tf_op jit(solution)/shard_map/all_to_all | solution.py:207
  58.6 0.0 copy-done.2
  58.6 5.2 %backward_map.1 = (f32[2,64,128]{2,1,0:T(8,128)S(1)}, f32[2,64,128]{2,1,0:T(8,128)S(1)}) custom-call(f32[512,512]{1,0:T(8,128)S(1)} %bitcast.10, bf16[512,512]{1,0:T(8,128)(2,1)S(1)} %get-tuple-element.19.n_high, bf16[512,512]{1,0:T(8,128)(2,1)S(1)} %get-tuple-element.20.n_low, f32[1,512]{1,0:T(1,128)S(1)} %bitcast.12, ...), custom_call_target="tpu_custom_call" | custom-call | tf_op jit(solution)/shard_map/backward_map/pallas_call | solution.py:210
  63.8 0.1 collective-permute-start.3
  63.9 1.2 %collective-permute-done.3 = f32[2,64,128]{2,1,0:T(8,128)S(1)} collective-permute-done((f32[2,64,128]{2,1,0:T(8,128)S(1)}, f32[2,64,128]{2,1,0:T(8,128)S(1)}, u32[]{:S(2)}, u32[]{:S(2)}) %collective-permute-start.3) | collective-permute-done | bytes 65568 | tf_op jit(solution)/shard_map/ppermute | solution.py:225
  65.2 2.6 %collective-permute-start.4 = (f32[64,128]{1,0:T(8,128)S(1)}, f32[64,128]{1,0:T(8,128)S(1)}, u32[]{:S(2)}, u32[]{:S(2)}) collective-permute-start(f32[64,128]{1,0:T(8,128)S(1)} %slice_bitcast_fusion), channel_id=1, source_target_pairs={{0,64},{32,96},{64,0},{96,32},{1,65},{33,97},{65,1},{97,33},{2,66}... | collective-permute-start | bytes 98312 | tf_op jit(solution)/shard_map/ppermute | solution.py:226
  67.7 2.9 %collective-permute-done.4 = f32[64,128]{1,0:T(8,128)S(1)} collective-permute-done((f32[64,128]{1,0:T(8,128)S(1)}, f32[64,128]{1,0:T(8,128)S(1)}, u32[]{:S(2)}, u32[]{:S(2)}) %collective-permute-start.4) | collective-permute-done | bytes 32800 | tf_op jit(solution)/shard_map/ppermute | solution.py:226
  70.7 0.6 fusion
  (2 shorter events, 0.0 us)
Async XLA Ops:
  0.0 6.9 %collective-permute-start.1 = (f32[64,128]{1,0:T(8,128)}, f32[64,128]{1,0:T(8,128)S(1)}, u32[]{:S(2)}, u32[]{:S(2)}) collective-permute-start(f32[64,128]{1,0:T(8,128)} %p0.1), channel_id=1, source_target_pairs={{0,64},{32,96},{64,0},{96,32},{1,65},{33,97},{65,1},{97,33},{2,66}... | collective-permute-start | bytes 98312 | tf_op jit(solution)/shard_map/ppermute | solution.py:152
  3.3 4.2 %collective-permute-start = (f32[64,128]{1,0:T(8,128)}, f32[64,128]{1,0:T(8,128)S(1)}, u32[]{:S(2)}, u32[]{:S(2)}) collective-permute-start(f32[64,128]{1,0:T(8,128)} %p0.1), channel_id=1, source_target_pairs={{0,32},{32,0},{64,96},{96,64},{1,33},{33,1},{65,97},{97,65},{2,34}... | collective-permute-start | bytes 98312 | tf_op jit(solution)/shard_map/ppermute | solution.py:153
  3.3 5.1 %copy-start = (f32[64,128]{1,0:T(8,128)S(1)}, f32[64,128]{1,0:T(8,128)}, u32[]{:S(2)}) copy-start(f32[64,128]{1,0:T(8,128)} %p0.1) | copy-start | bytes 98308
  3.3 5.1 %copy-start.1 = (f32[64,64]{1,0:T(8,128)S(1)}, f32[64,64]{1,0:T(8,128)}, u32[]{:S(2)}) copy-start(f32[64,64]{1,0:T(8,128)} %noise.1) | copy-start | bytes 49156
  6.9 1.4 %collective-permute-start.2 = (f32[64,128]{1,0:T(8,128)S(1)}, f32[64,128]{1,0:T(8,128)S(1)}, u32[]{:S(2)}, u32[]{:S(2)}) collective-permute-start(f32[64,128]{1,0:T(8,128)S(1)} %collective-permute-done.1.p2), channel_id=1, source_target_pairs={{0,32},{32,0},{64,96},{96,64},{1,33},{33,1},{65,97},{97,65},{2,34}... | collective-permute-start | bytes 98312 | tf_op jit(solution)/shard_map/ppermute | solution.py:176
  37.8 20.8 %copy-start.2 = (f32[512]{0:T(512)S(1)}, f32[512]{0:T(512)}, u32[]{:S(2)}) copy-start(f32[512]{0:T(512)} %param.7) | copy-start | bytes 6148
  63.8 1.3 %collective-permute-start.3 = (f32[2,64,128]{2,1,0:T(8,128)S(1)}, f32[2,64,128]{2,1,0:T(8,128)S(1)}, u32[]{:S(2)}, u32[]{:S(2)}) collective-permute-start(f32[2,64,128]{2,1,0:T(8,128)S(1)} %get-tuple-element.22), channel_id=1, source_target_pairs={{0,32},{32,0},{64,96},{96,64},{1,33},{33,1},{65,97},{97,65},{2,34}... | collective-permute-start | bytes 196616 | tf_op jit(solution)/shard_map/ppermute | solution.py:225
  65.2 5.5 %collective-permute-start.4 = (f32[64,128]{1,0:T(8,128)S(1)}, f32[64,128]{1,0:T(8,128)S(1)}, u32[]{:S(2)}, u32[]{:S(2)}) collective-permute-start(f32[64,128]{1,0:T(8,128)S(1)} %slice_bitcast_fusion), channel_id=1, source_target_pairs={{0,64},{32,96},{64,0},{96,32},{1,65},{33,97},{65,1},{97,33},{2,66}... | collective-permute-start | bytes 98312 | tf_op jit(solution)/shard_map/ppermute | solution.py:226

commit v5 on v4

--- a/solution.py
+++ b/solution.py
@@ -9,7 +9,6 @@
 BF16 = jnp.bfloat16
 GROUP = 4
 PIECES = 8
-NOISE_ROWS = 128
 
 
 def split(value):
@@ -41,27 +40,11 @@
         k_low[rows, :] = low
 
 
-def widen_noise(noise, wide_refs):
-    time_steps = noise.shape[0]
-    columns = wide_refs[0].shape[0]
-    row = lax.broadcasted_iota(jnp.int32, (time_steps, columns), 0)
-    col = lax.broadcasted_iota(jnp.int32, (time_steps, columns), 1)
-    expand = jnp.where(row == col // 8, 1.0, 0.0).astype(BF16)
-    same = (
-        lax.broadcasted_iota(jnp.int32, (1, 8, columns), 1)
-        == lax.broadcasted_iota(jnp.int32, (1, 8, columns), 2) % 8
-    )
-    for part, wide_ref in zip(split(noise[...]), wide_refs):
-        wide = jnp.dot(part, expand, preferred_element_type=F32)
-        wide = jnp.where(same, wide[:, None, :], 0.0)
-        wide_ref[...] = wide.reshape(columns, columns).astype(BF16)
-
-
 def forward_kernel(
-    p0, p1, p2, p3, noise, k_high, k_low, out_ref, n_high, n_low, field, f_high, f_low
+    p0, p1, p2, p3, k_high, k_low, out_ref, field, f_high, f_low, sums
 ):
     params, part_columns = p0.shape
-    columns = out_ref.shape[0]
+    blocks, columns, width = sums.shape
     block_rows = GROUP * params
     step_rows = 8 * GROUP
     me = lax.axis_index("sens")
@@ -73,7 +56,6 @@
         [field[pl.ds(step_rows - 8 * lag, columns), :] for lag in range(GROUP)], axis=1
     )
     f_high[...], f_low[...] = split(shifted)
-    widen_noise(noise, (n_high, n_low))
     for b in range(k_high.shape[0] // block_rows):
         rows = pl.ds(b * block_rows, block_rows)
         source = pl.ds(0, columns - step_rows * b)
@@ -82,35 +64,50 @@
         both = jnp.dot(both, k_high[rows, :], preferred_element_type=F32)
         term = both[: source.size] + both[source.size :]
         term += jnp.dot(f_high[source, :], k_low[rows, :], preferred_element_type=F32)
-        if b == 0:
-            out_ref[target, :] = term
-        else:
-            out_ref[target, :] += term
-
-
-def share_kernel(pieces, k_high, k_low, out_ref):
+        for block in range(blocks):
+            part = term[:, block * width : (block + 1) * width]
+            if b == 0:
+                sums[block, target, :] = part
+            else:
+                sums[block, target, :] += part
+
+
+    for part, place in parts_of(out_ref):
+        out_ref[part] = sums[place]
+
+
+def parts_of(pieces):
+    count, time_steps, _ = pieces.shape
+    for part in range(count):
+        probe, block = divmod(part, count // 8)
+        yield part, (block, pl.ds(probe, time_steps, stride=8), slice(None))
+
+
+def share_kernel(pieces, noise, sensor_weight, k_high, k_low, out_ref):
     del k_high, k_low
-    total = jnp.sum(pieces[...], axis=0)
-    for part in range(out_ref.shape[0]):
-        out_ref[part] = total
-
-
-def backward_kernel(
-    observed, n_high, n_low, sensor_weight, k_high, k_low, kept, sent,
-    spread, w_high, w_low, o_high, o_low,
-):
-    columns, sensors = observed.shape
+    count, _, width = pieces.shape
+    high, low = split(jnp.sum(pieces[...], axis=0))
+    n_high, n_low = split(noise[...])
+    mixed = jnp.dot(n_high, high, preferred_element_type=F32)
+    mixed += jnp.dot(n_high, low, preferred_element_type=F32)
+    mixed += jnp.dot(n_low, high, preferred_element_type=F32)
+    block = lax.rem(lax.axis_index("par"), count // 8)
+    mixed *= sensor_weight[:, pl.ds(pl.multiple_of(block * width, width), width)]
+    for part in range(count):
+        out_ref[part] = mixed
+
+
+def backward_kernel(pieces, k_high, k_low, kept, sent, whole, spread, w_high, w_low):
+    blocks, columns, width = whole.shape
     params = kept.shape[1]
     part_columns = kept.shape[2]
     block_rows = GROUP * params
     step_rows = 8 * GROUP
-    o_high[...], o_low[...] = split(observed[...])
-    for start in range(0, columns, NOISE_ROWS):
-        rows = pl.ds(start, NOISE_ROWS)
-        mixed = jnp.dot(n_high[rows, :], o_high[...], preferred_element_type=F32)
-        mixed += jnp.dot(n_high[rows, :], o_low[...], preferred_element_type=F32)
-        mixed += jnp.dot(n_low[rows, :], o_high[...], preferred_element_type=F32)
-        w_high[rows, :], w_low[rows, :] = split(mixed * sensor_weight[...])
+    for part, place in parts_of(pieces):
+        whole[place] = pieces[part]
+    for block in range(blocks):
+        lanes = pl.ds(block * width, width)
+        w_high[:, lanes], w_low[:, lanes] = split(whole[block])
     spread[pl.ds(columns, step_rows), :] = jnp.zeros((step_rows, block_rows), F32)
     for b in range(k_high.shape[0] // block_rows):
         rows = pl.ds(b * block_rows, block_rows)
@@ -153,7 +150,6 @@
     beside = lax.ppermute(probes, "sens", swap_core)
 
     half_kernel = jax.ShapeDtypeStruct((kernel_rows, sensors), BF16)
-    half_noise = jax.ShapeDtypeStruct((columns, columns), BF16)
     k_high, k_low = pl.pallas_call(
         prepare_kernel,
         out_shape=(half_kernel, half_kernel),
@@ -175,53 +171,49 @@
     across, k_high = lax.optimization_barrier((across, k_high))
     diagonal = lax.ppermute(across, "sens", swap_core)
 
-    partial, n_high, n_low = pl.pallas_call(
+    blocks = par // 8
+    shape = jax.ShapeDtypeStruct((par, time_steps, sensors // blocks), F32)
+    partial = pl.pallas_call(
         forward_kernel,
-        out_shape=(
-            jax.ShapeDtypeStruct((columns, sensors), F32),
-            half_noise,
-            half_noise,
-        ),
-        in_specs=[vmem] * 7,
-        out_specs=(vmem,) * 3,
+        out_shape=shape,
+        in_specs=[vmem] * 6,
+        out_specs=vmem,
         scratch_shapes=[
             pltpu.VMEM((step_rows + columns, params), F32),
             pltpu.VMEM((columns, block_rows), BF16),
             pltpu.VMEM((columns, block_rows), BF16),
+            pltpu.VMEM((blocks, columns, sensors // blocks), F32),
         ],
         compiler_params=compiler_params,
         name="forward_map",
-    )(probes, beside, across, diagonal, noise_inverse, k_high, k_low)
-
-    pieces = lax.all_to_all(
-        partial.reshape(par, columns // par, sensors), "par", 0, 0, tiled=True
-    )
+    )(probes, beside, across, diagonal, k_high, k_low)
+
+    pieces = lax.all_to_all(partial, "par", 0, 0, tiled=True)
     shares = pl.pallas_call(
         share_kernel,
-        out_shape=jax.ShapeDtypeStruct(pieces.shape, F32),
-        in_specs=[vmem] * 3,
+        out_shape=shape,
+        in_specs=[vmem] * 5,
         out_specs=vmem,
         compiler_params=compiler_params,
         name="share",
-    )(pieces, k_high, k_low)
-    observed = lax.all_to_all(shares, "par", 0, 0, tiled=True).reshape(columns, sensors)
+    )(pieces, noise_inverse, sensor_weight.reshape(1, sensors), k_high, k_low)
+    weighted = lax.all_to_all(shares, "par", 0, 0, tiled=True)
 
     piece = jax.ShapeDtypeStruct((2, params, part_columns), F32)
     kept, sent = pl.pallas_call(
         backward_kernel,
         out_shape=(piece, piece),
-        in_specs=[vmem] * 6,
+        in_specs=[vmem] * 3,
         out_specs=(vmem, vmem),
         scratch_shapes=[
+            pltpu.VMEM((blocks, columns, sensors // blocks), F32),
             pltpu.VMEM((columns + step_rows, block_rows), F32),
-            pltpu.VMEM((columns, sensors), BF16),
-            pltpu.VMEM((columns, sensors), BF16),
             pltpu.VMEM((columns, sensors), BF16),
             pltpu.VMEM((columns, sensors), BF16),
         ],
         compiler_params=compiler_params,
         name="backward_map",
-    )(observed, n_high, n_low, sensor_weight.reshape(1, sensors), k_high, k_low)
+    )(weighted, k_high, k_low)
     kept += lax.ppermute(sent, "sens", swap_core)
     return kept[0] + lax.ppermute(kept[1], "sens", swap_chip)
 

time: 71.5 us -> 70.8 us (level)
    pallas_call x1, Pallas kernels: 5.25 us -> 4.42 us  [per_device(): pl.pallas_call(backward_kernel, out_shape=(piece, piece), in_specs=[vmem]...]
where the time goes in v5:
time: 70.8 us; the launch traced here: 70.7 us
  blocking collectives  46.1 us (65%)
  Pallas kernels  12.3 us (17%)
  starting transfers between devices  6.51 us (9%)
  waiting for transfers between devices  5.04 us (7%)
    all_to_all x1, blocking collectives, per_device(): pieces = lax.all_to_all(partial, 'par', 0, 0, tiled=True)  25.5 us
    all_to_all x1, blocking collectives, per_device(): weighted = lax.all_to_all(shares, 'par', 0, 0, tiled=True)  20.6 us
    pallas_call x1, Pallas kernels, per_device(): pl.pallas_call(backward_kernel, out_shape=(piece, piece), in_specs=[vmem]...  4.42 us
    pallas_call x1, Pallas kernels, per_device(): pl.pallas_call(forward_kernel, out_shape=shape, in_specs=[vmem] * 6, out_...  3.94 us
    pallas_call x1, Pallas kernels, per_device(): pl.pallas_call(prepare_kernel, out_shape=(half_kernel, half_kernel), in_s...  3.61 us
    ppermute x1, starting transfers between devices, per_device(): across = lax.ppermute(probes, 'sens', swap_chip)  3.28 us
    ppermute x1, waiting for transfers between devices, per_device(): return kept[0] + lax.ppermute(kept[1], 'sens', swap_chip)  2.94 us
    ppermute x1, starting transfers between devices, per_device(): return kept[0] + lax.ppermute(kept[1], 'sens', swap_chip)  2.56 us
  transfers between devices with their start and end apart: 5, of which 3 were waited for; matrix products, arithmetic and copies ran while one was open for 0% of the time, Pallas kernels for 5%

profile of v5, /device:TPU:0, one launch (start us, length us, event | category | flops | bytes accessed | tf_op | source)
XLA Modules:
  0.0 70.7 jit_solution(7019603249617886648)
XLA Ops:
  0.0 3.3 %collective-permute-start.1 = (f32[64,128]{1,0:T(8,128)}, f32[64,128]{1,0:T(8,128)S(1)}, u32[]{:S(2)}, u32[]{:S(2)}) collective-permute-start(f32[64,128]{1,0:T(8,128)} %p0.1), channel_id=1, source_target_pairs={{0,64},{32,96},{64,0},{96,32},{1,65},{33,97},{65,1},{97,33},{2,66}... | collective-permute-start | bytes 98312 | tf_op jit(solution)/shard_map/ppermute | solution.py:149
  3.3 0.0 collective-permute-start
  3.3 0.0 copy-start
  3.3 3.6 %prepare.1 = (bf16[4096,512]{1,0:T(8,128)(2,1)S(1)}, bf16[4096,512]{1,0:T(8,128)(2,1)S(1)}) custom-call(f32[4096,512]{1,0:T(8,128)} %bitcast.9), custom_call_target="tpu_custom_call" | custom-call | flops 16777216 | bytes 16777216 | tf_op jit(solution)/shard_map/prepare/pallas_call | solution.py:153
  6.9 0.0 collective-permute-done.1.p2
  6.9 0.6 collective-permute-start.2
  7.5 0.0 collective-permute-done.p1
  7.5 0.9 %collective-permute-done.2.p3 = f32[64,128]{1,0:T(8,128)S(1)} collective-permute-done((f32[64,128]{1,0:T(8,128)S(1)}, f32[64,128]{1,0:T(8,128)S(1)}, u32[]{:S(2)}, u32[]{:S(2)}) %collective-permute-start.2) | collective-permute-done | bytes 32800 | tf_op jit(solution)/shard_map/ppermute | solution.py:172
  8.4 0.0 copy-done
  8.4 0.0 copy-start.1
  8.4 0.0 copy-start.2
  8.4 3.9 %forward_map.1 = f32[32,64,128]{2,1,0:T(8,128)S(1)} custom-call(f32[64,128]{1,0:T(8,128)S(1)} %copy-done, f32[64,128]{1,0:T(8,128)S(1)} %collective-permute-done.p1, f32[64,128]{1,0:T(8,128)S(1)} %collective-permute-done.1.p2, f32[64,128]{1,0:T(8,128)S(1)} %collective-permute-done.2.p3, bf16[4096,512]{1,0:T(8,128)(2,1)S(1)} %get-tuple-element.13.k_high, ...), custom_call_target="tpu_custom_call" | custom-call | tf_op jit(solution)/shard_map/forward_map/pallas_call | solution.py:176
  12.3 25.5 %all_to_all.10.pieces = f32[32,64,128]{2,1,0:T(8,128)S(1)} all-to-all(f32[32,64,128]{2,1,0:T(8,128)S(1)} %forward_map.1), channel_id=1, replica_groups=mesh['sens'=4,'par'=32] {'par'}, dimensions={0} | all-to-all | bytes 2097152 | tf_op jit(solution)/shard_map/all_to_all | solution.py:191
  37.8 0.0 copy-done.1
  37.8 0.0 copy-done.2
  37.8 0.3 share.1
  38.1 20.6 %all_to_all.11.pieces = f32[32,64,128]{2,1,0:T(8,128)S(1)} all-to-all(f32[32,64,128]{2,1,0:T(8,128)S(1)} %share.1), channel_id=1, replica_groups=mesh['sens'=4,'par'=32] {'par'}, dimensions={0} | all-to-all | bytes 2097152 | tf_op jit(solution)/shard_map/all_to_all | solution.py:200
  58.8 4.4 %backward_map.1 = (f32[2,64,128]{2,1,0:T(8,128)S(1)}, f32[2,64,128]{2,1,0:T(8,128)S(1)}) custom-call(f32[32,64,128]{2,1,0:T(8,128)S(1)} %all_to_all.11.pieces, bf16[4096,512]{1,0:T(8,128)(2,1)S(1)} %get-tuple-element.13.k_high, bf16[4096,512]{1,0:T(8,128)(2,1)S(1)} %get-tuple-element.14.k_low), custom_call_target="tpu_custom_call" | custom-call | tf_op jit(solution)/shard_map/backward_map/pallas_call | solution.py:203
  63.2 0.1 collective-permute-start.3
  63.3 1.2 %collective-permute-done.3 = f32[2,64,128]{2,1,0:T(8,128)S(1)} collective-permute-done((f32[2,64,128]{2,1,0:T(8,128)S(1)}, f32[2,64,128]{2,1,0:T(8,128)S(1)}, u32[]{:S(2)}, u32[]{:S(2)}) %collective-permute-start.3) | collective-permute-done | bytes 65568 | tf_op jit(solution)/shard_map/ppermute | solution.py:217
  64.6 2.6 %collective-permute-start.4 = (f32[64,128]{1,0:T(8,128)S(1)}, f32[64,128]{1,0:T(8,128)S(1)}, u32[]{:S(2)}, u32[]{:S(2)}) collective-permute-start(f32[64,128]{1,0:T(8,128)S(1)} %slice_bitcast_fusion), channel_id=1, source_target_pairs={{0,64},{32,96},{64,0},{96,32},{1,65},{33,97},{65,1},{97,33},{2,66}... | collective-permute-start | bytes 98312 | tf_op jit(solution)/shard_map/ppermute | solution.py:218
  67.1 2.9 %collective-permute-done.4 = f32[64,128]{1,0:T(8,128)S(1)} collective-permute-done((f32[64,128]{1,0:T(8,128)S(1)}, f32[64,128]{1,0:T(8,128)S(1)}, u32[]{:S(2)}, u32[]{:S(2)}) %collective-permute-start.4) | collective-permute-done | bytes 32800 | tf_op jit(solution)/shard_map/ppermute | solution.py:218
  70.0 0.6 fusion
  (2 shorter events, 0.0 us)
Async XLA Ops:
  0.0 6.9 %collective-permute-start.1 = (f32[64,128]{1,0:T(8,128)}, f32[64,128]{1,0:T(8,128)S(1)}, u32[]{:S(2)}, u32[]{:S(2)}) collective-permute-start(f32[64,128]{1,0:T(8,128)} %p0.1), channel_id=1, source_target_pairs={{0,64},{32,96},{64,0},{96,32},{1,65},{33,97},{65,1},{97,33},{2,66}... | collective-permute-start | bytes 98312 | tf_op jit(solution)/shard_map/ppermute | solution.py:149
  3.3 4.2 %collective-permute-start = (f32[64,128]{1,0:T(8,128)}, f32[64,128]{1,0:T(8,128)S(1)}, u32[]{:S(2)}, u32[]{:S(2)}) collective-permute-start(f32[64,128]{1,0:T(8,128)} %p0.1), channel_id=1, source_target_pairs={{0,32},{32,0},{64,96},{96,64},{1,33},{33,1},{65,97},{97,65},{2,34}... | collective-permute-start | bytes 98312 | tf_op jit(solution)/shard_map/ppermute | solution.py:150
  3.3 5.1 %copy-start = (f32[64,128]{1,0:T(8,128)S(1)}, f32[64,128]{1,0:T(8,128)}, u32[]{:S(2)}) copy-start(f32[64,128]{1,0:T(8,128)} %p0.1) | copy-start | bytes 98308
  6.9 1.4 %collective-permute-start.2 = (f32[64,128]{1,0:T(8,128)S(1)}, f32[64,128]{1,0:T(8,128)S(1)}, u32[]{:S(2)}, u32[]{:S(2)}) collective-permute-start(f32[64,128]{1,0:T(8,128)S(1)} %collective-permute-done.1.p2), channel_id=1, source_target_pairs={{0,32},{32,0},{64,96},{96,64},{1,33},{33,1},{65,97},{97,65},{2,34}... | collective-permute-start | bytes 98312 | tf_op jit(solution)/shard_map/ppermute | solution.py:172
  8.4 29.5 %copy-start.1 = (f32[64,64]{1,0:T(8,128)S(1)}, f32[64,64]{1,0:T(8,128)}, u32[]{:S(2)}) copy-start(f32[64,64]{1,0:T(8,128)} %noise.1) | copy-start | bytes 49156
  8.4 29.5 %copy-start.2 = (f32[512]{0:T(512)S(1)}, f32[512]{0:T(512)}, u32[]{:S(2)}) copy-start(f32[512]{0:T(512)} %param.7) | copy-start | bytes 6148
  63.2 1.3 %collective-permute-start.3 = (f32[2,64,128]{2,1,0:T(8,128)S(1)}, f32[2,64,128]{2,1,0:T(8,128)S(1)}, u32[]{:S(2)}, u32[]{:S(2)}) collective-permute-start(f32[2,64,128]{2,1,0:T(8,128)S(1)} %get-tuple-element.16), channel_id=1, source_target_pairs={{0,32},{32,0},{64,96},{96,64},{1,33},{33,1},{65,97},{97,65},{2,34}... | collective-permute-start | bytes 196616 | tf_op jit(solution)/shard_map/ppermute | solution.py:217
  64.6 5.5 %collective-permute-start.4 = (f32[64,128]{1,0:T(8,128)S(1)}, f32[64,128]{1,0:T(8,128)S(1)}, u32[]{:S(2)}, u32[]{:S(2)}) collective-permute-start(f32[64,128]{1,0:T(8,128)S(1)} %slice_bitcast_fusion), channel_id=1, source_target_pairs={{0,64},{32,96},{64,0},{96,32},{1,65},{33,97},{65,1},{97,33},{2,66}... | collective-permute-start | bytes 98312 | tf_op jit(solution)/shard_map/ppermute | solution.py:218

commit v6 on v5

--- a/solution.py
+++ b/solution.py
@@ -97,10 +97,11 @@
         out_ref[part] = mixed
 
 
-def backward_kernel(pieces, k_high, k_low, kept, sent, whole, spread, w_high, w_low):
+def backward_kernel(
+    pieces, k_high, k_low, kept, sent, kept_far, sent_far, whole, spread, w_high, w_low
+):
     blocks, columns, width = whole.shape
-    params = kept.shape[1]
-    part_columns = kept.shape[2]
+    params, part_columns = kept.shape
     block_rows = GROUP * params
     step_rows = 8 * GROUP
     for part, place in parts_of(pieces):
@@ -123,7 +124,7 @@
             spread[target, :] += term
 
     me = lax.axis_index("sens")
-    for other, target in enumerate((kept.at[0], sent.at[0], kept.at[1], sent.at[1])):
+    for other, target in enumerate((kept, sent, kept_far, sent_far)):
         start = pl.multiple_of(part_columns * jnp.bitwise_xor(me, other), part_columns)
         total = spread[pl.ds(start, part_columns), pl.ds(0, params)]
         for lag in range(1, GROUP):
@@ -199,12 +200,12 @@
     )(pieces, noise_inverse, sensor_weight.reshape(1, sensors), k_high, k_low)
     weighted = lax.all_to_all(shares, "par", 0, 0, tiled=True)
 
-    piece = jax.ShapeDtypeStruct((2, params, part_columns), F32)
-    kept, sent = pl.pallas_call(
+    piece = jax.ShapeDtypeStruct((params, part_columns), F32)
+    kept, sent, kept_far, sent_far = pl.pallas_call(
         backward_kernel,
-        out_shape=(piece, piece),
+        out_shape=(piece,) * 4,
         in_specs=[vmem] * 3,
-        out_specs=(vmem, vmem),
+        out_specs=(vmem,) * 4,
         scratch_shapes=[
             pltpu.VMEM((blocks, columns, sensors // blocks), F32),
             pltpu.VMEM((columns + step_rows, block_rows), F32),
@@ -214,8 +215,10 @@
         compiler_params=compiler_params,
         name="backward_map",
     )(weighted, k_high, k_low)
-    kept += lax.ppermute(sent, "sens", swap_core)
-    return kept[0] + lax.ppermute(kept[1], "sens", swap_chip)
+    far = kept_far + lax.ppermute(sent_far, "sens", swap_core)
+    near = lax.ppermute(sent, "sens", swap_core)
+    far = lax.ppermute(far, "sens", swap_chip)
+    return kept + near + far
 
 
 def solution(mesh):

time: 70.8 us -> 70.7 us (level)
    ppermute x2 -> x3, waiting for transfers between devices: 4.18 us -> 3.63 us  [the longest x1 2.93 us: per_device(): far = lax.ppermute(far, 'sens', swap_chip)]
    ppermute x2 -> x3, starting transfers between devices: 2.64 us -> 3.06 us  [the longest x1 2.48 us: per_device(): far = lax.ppermute(far, 'sens', swap_chip)]
  transfers between devices with their start and end apart: 5 -> 6, of which waited for: 3 -> 3; matrix products, arithmetic and copies ran while one was open for 0% -> 0% of each run, Pallas kernels for 5% -> 5%
where the time goes in v6:
time: 70.7 us; the launch traced here: 70.5 us
  blocking collectives  46.1 us (65%)
  Pallas kernels  12.3 us (17%)
  starting transfers between devices  6.93 us (10%)
  waiting for transfers between devices  4.5 us (6%)
    all_to_all x1, blocking collectives, per_device(): pieces = lax.all_to_all(partial, 'par', 0, 0, tiled=True)  25.5 us
    all_to_all x1, blocking collectives, per_device(): weighted = lax.all_to_all(shares, 'par', 0, 0, tiled=True)  20.6 us
    pallas_call x1, Pallas kernels, per_device(): pl.pallas_call(backward_kernel, out_shape=(piece,) * 4, in_specs=[vmem] *...  4.42 us
    pallas_call x1, Pallas kernels, per_device(): pl.pallas_call(forward_kernel, out_shape=shape, in_specs=[vmem] * 6, out_...  3.94 us
    pallas_call x1, Pallas kernels, per_device(): pl.pallas_call(prepare_kernel, out_shape=(half_kernel, half_kernel), in_s...  3.61 us
    ppermute x1, starting transfers between devices, per_device(): across = lax.ppermute(probes, 'sens', swap_chip)  3.28 us
    ppermute x1, waiting for transfers between devices, per_device(): far = lax.ppermute(far, 'sens', swap_chip)  2.93 us
    ppermute x1, starting transfers between devices, per_device(): far = lax.ppermute(far, 'sens', swap_chip)  2.48 us
  transfers between devices with their start and end apart: 6, of which 3 were waited for; matrix products, arithmetic and copies ran while one was open for 0% of the time, Pallas kernels for 5%

profile of v6, /device:TPU:0, one launch (start us, length us, event | category | flops | bytes accessed | tf_op | source)
XLA Modules:
  0.0 70.5 jit_solution(11263867269534175636)
XLA Ops:
  0.0 3.3 %collective-permute-start.1 = (f32[64,128]{1,0:T(8,128)}, f32[64,128]{1,0:T(8,128)S(1)}, u32[]{:S(2)}, u32[]{:S(2)}) collective-permute-start(f32[64,128]{1,0:T(8,128)} %p0.1), channel_id=1, source_target_pairs={{0,64},{32,96},{64,0},{96,32},{1,65},{33,97},{65,1},{97,33},{2,66}... | collective-permute-start | bytes 98312 | tf_op jit(solution)/shard_map/ppermute | solution.py:150
  3.3 0.0 collective-permute-start
  3.3 0.0 copy-start
  3.3 3.6 %prepare.1 = (bf16[4096,512]{1,0:T(8,128)(2,1)S(1)}, bf16[4096,512]{1,0:T(8,128)(2,1)S(1)}) custom-call(f32[4096,512]{1,0:T(8,128)} %bitcast.3), custom_call_target="tpu_custom_call" | custom-call | flops 16777216 | bytes 16777216 | tf_op jit(solution)/shard_map/prepare/pallas_call | solution.py:154
  6.9 0.0 collective-permute-done.1.p2
  6.9 0.6 collective-permute-start.2
  7.5 0.0 collective-permute-done.p1
  7.5 0.9 %collective-permute-done.2.p3 = f32[64,128]{1,0:T(8,128)S(1)} collective-permute-done((f32[64,128]{1,0:T(8,128)S(1)}, f32[64,128]{1,0:T(8,128)S(1)}, u32[]{:S(2)}, u32[]{:S(2)}) %collective-permute-start.2) | collective-permute-done | bytes 32800 | tf_op jit(solution)/shard_map/ppermute | solution.py:173
  8.4 0.0 copy-done
  8.4 0.0 copy-start.1
  8.4 3.9 %forward_map.1 = f32[32,64,128]{2,1,0:T(8,128)S(1)} custom-call(f32[64,128]{1,0:T(8,128)S(1)} %copy-done, f32[64,128]{1,0:T(8,128)S(1)} %collective-permute-done.p1, f32[64,128]{1,0:T(8,128)S(1)} %collective-permute-done.1.p2, f32[64,128]{1,0:T(8,128)S(1)} %collective-permute-done.2.p3, bf16[4096,512]{1,0:T(8,128)(2,1)S(1)} %get-tuple-element.15.k_high, ...), custom_call_target="tpu_custom_call" | custom-call | tf_op jit(solution)/shard_map/forward_map/pallas_call | solution.py:177
  12.3 25.5 %all_to_all.10.pieces = f32[32,64,128]{2,1,0:T(8,128)S(1)} all-to-all(f32[32,64,128]{2,1,0:T(8,128)S(1)} %forward_map.1), channel_id=1, replica_groups=mesh['sens'=4,'par'=32] {'par'}, dimensions={0} | all-to-all | bytes 2097152 | tf_op jit(solution)/shard_map/all_to_all | solution.py:192
  37.8 0.0 copy-done.1
  37.8 0.0 copy-done.2
  37.8 0.3 share.1
  38.1 20.6 %all_to_all.11.pieces = f32[32,64,128]{2,1,0:T(8,128)S(1)} all-to-all(f32[32,64,128]{2,1,0:T(8,128)S(1)} %share.1), channel_id=1, replica_groups=mesh['sens'=4,'par'=32] {'par'}, dimensions={0} | all-to-all | bytes 2097152 | tf_op jit(solution)/shard_map/all_to_all | solution.py:201
  58.8 4.4 %backward_map.1 = (f32[64,128]{1,0:T(8,128)S(1)}, f32[64,128]{1,0:T(8,128)S(1)}, f32[64,128]{1,0:T(8,128)S(1)}, f32[64,128]{1,0:T(8,128)S(1)}) custom-call(f32[32,64,128]{2,1,0:T(8,128)S(1)} %all_to_all.11.pieces, bf16[4096,512]{1,0:T(8,128)(2,1)S(1)} %get-tuple-element.15.k_high, bf16[4096,512]{1,0:T(8,128)(2,1)S(1)} %get-tuple-element.16.k_low), custom_call_target="tpu_custom_call" | custom-call | tf_op jit(solution)/shard_map/backward_map/pallas_call | solution.py:204
  63.2 0.1 collective-permute-start.4
  63.3 0.5 collective-permute-start.3
  63.8 0.7 collective-permute-done.4
  64.5 2.5 %collective-permute-start.5 = (f32[64,128]{1,0:T(8,128)S(1)}, f32[64,128]{1,0:T(8,128)S(1)}, u32[]{:S(2)}, u32[]{:S(2)}) collective-permute-start(f32[64,128]{1,0:T(8,128)S(1)} %add.10), channel_id=1, source_target_pairs={{0,64},{32,96},{64,0},{96,32},{1,65},{33,97},{65,1},{97,33},{2,66}... | collective-permute-start | bytes 98312 | tf_op jit(solution)/shard_map/ppermute | solution.py:220
  67.0 0.0 collective-permute-done.3
  67.0 2.9 %collective-permute-done.5 = f32[64,128]{1,0:T(8,128)S(1)} collective-permute-done((f32[64,128]{1,0:T(8,128)S(1)}, f32[64,128]{1,0:T(8,128)S(1)}, u32[]{:S(2)}, u32[]{:S(2)}) %collective-permute-start.5) | collective-permute-done | bytes 32800 | tf_op jit(solution)/shard_map/ppermute | solution.py:220
  69.9 0.6 add_add_fusion
  (2 shorter events, 0.0 us)
Async XLA Ops:
  0.0 6.9 %collective-permute-start.1 = (f32[64,128]{1,0:T(8,128)}, f32[64,128]{1,0:T(8,128)S(1)}, u32[]{:S(2)}, u32[]{:S(2)}) collective-permute-start(f32[64,128]{1,0:T(8,128)} %p0.1), channel_id=1, source_target_pairs={{0,64},{32,96},{64,0},{96,32},{1,65},{33,97},{65,1},{97,33},{2,66}... | collective-permute-start | bytes 98312 | tf_op jit(solution)/shard_map/ppermute | solution.py:150
  3.3 4.2 %collective-permute-start = (f32[64,128]{1,0:T(8,128)}, f32[64,128]{1,0:T(8,128)S(1)}, u32[]{:S(2)}, u32[]{:S(2)}) collective-permute-start(f32[64,128]{1,0:T(8,128)} %p0.1), channel_id=1, source_target_pairs={{0,32},{32,0},{64,96},{96,64},{1,33},{33,1},{65,97},{97,65},{2,34}... | collective-permute-start | bytes 98312 | tf_op jit(solution)/shard_map/ppermute | solution.py:151
  3.3 5.1 %copy-start = (f32[64,128]{1,0:T(8,128)S(1)}, f32[64,128]{1,0:T(8,128)}, u32[]{:S(2)}) copy-start(f32[64,128]{1,0:T(8,128)} %p0.1) | copy-start | bytes 98308
  6.9 1.4 %collective-permute-start.2 = (f32[64,128]{1,0:T(8,128)S(1)}, f32[64,128]{1,0:T(8,128)S(1)}, u32[]{:S(2)}, u32[]{:S(2)}) collective-permute-start(f32[64,128]{1,0:T(8,128)S(1)} %collective-permute-done.1.p2), channel_id=1, source_target_pairs={{0,32},{32,0},{64,96},{96,64},{1,33},{33,1},{65,97},{97,65},{2,34}... | collective-permute-start | bytes 98312 | tf_op jit(solution)/shard_map/ppermute | solution.py:173
  8.4 29.5 %copy-start.1 = (f32[64,64]{1,0:T(8,128)S(1)}, f32[64,64]{1,0:T(8,128)}, u32[]{:S(2)}) copy-start(f32[64,64]{1,0:T(8,128)} %noise.1) | copy-start | bytes 49156
  8.4 29.5 %copy-start.2 = (f32[512]{0:T(512)S(1)}, f32[512]{0:T(512)}, u32[]{:S(2)}) copy-start(f32[512]{0:T(512)} %param.7) | copy-start | bytes 6148
  63.2 1.3 %collective-permute-start.4 = (f32[64,128]{1,0:T(8,128)S(1)}, f32[64,128]{1,0:T(8,128)S(1)}, u32[]{:S(2)}, u32[]{:S(2)}) collective-permute-start(f32[64,128]{1,0:T(8,128)S(1)} %get-tuple-element.20), channel_id=1, source_target_pairs={{0,32},{32,0},{64,96},{96,64},{1,33},{33,1},{65,97},{97,65},{2,34}... | collective-permute-start | bytes 98312 | tf_op jit(solution)/shard_map/ppermute | solution.py:218
  63.3 3.7 %collective-permute-start.3 = (f32[64,128]{1,0:T(8,128)S(1)}, f32[64,128]{1,0:T(8,128)S(1)}, u32[]{:S(2)}, u32[]{:S(2)}) collective-permute-start(f32[64,128]{1,0:T(8,128)S(1)} %get-tuple-element.18), channel_id=1, source_target_pairs={{0,32},{32,0},{64,96},{96,64},{1,33},{33,1},{65,97},{97,65},{2,34}... | collective-permute-start | bytes 98312 | tf_op jit(solution)/shard_map/ppermute | solution.py:219
  64.5 5.4 %collective-permute-start.5 = (f32[64,128]{1,0:T(8,128)S(1)}, f32[64,128]{1,0:T(8,128)S(1)}, u32[]{:S(2)}, u32[]{:S(2)}) collective-permute-start(f32[64,128]{1,0:T(8,128)S(1)} %add.10), channel_id=1, source_target_pairs={{0,64},{32,96},{64,0},{96,32},{1,65},{33,97},{65,1},{97,33},{2,66}... | collective-permute-start | bytes 98312 | tf_op jit(solution)/shard_map/ppermute | solution.py:220
